TPU v7x, 256 devices: a whole 4x4x8 slice. The times are simulated.
256 devices in a mesh: dp: 4 (over x), ctx: 64 (over z, y, core).
Axes of the slice: x: 4, y: 4, z: 8, core: 2. Of those that a mesh axis runs over, the one named last changes fastest.
Arguments:
- query_in: bfloat16 [4, 16384, 2048], P('dp', 'ctx'), may hold values from -68 to 68
- key_in: bfloat16 [4, 16384, 2048], P('dp', 'ctx'), may hold values from -6 to 6
- value_in: bfloat16 [4, 16384, 2048], P('dp', 'ctx'), may hold values from -6 to 6
- conv_weight: float32 [3, 4, 2048], replicated, may hold values from -3 to 3
- out_grad: bfloat16 [4, 16384, 2048], P('dp', 'ctx'), may hold values from -6 to 6
- block_lists: int32 [4, 256, 16], P('dp', 'ctx'), may hold values from 0 to 255, as said below
Outputs:
- query_in_grad: bfloat16 [4, 16384, 2048], P('dp', 'ctx')
- key_in_grad: bfloat16 [4, 16384, 2048], P('dp', 'ctx')
- value_in_grad: bfloat16 [4, 16384, 2048], P('dp', 'ctx')
- conv_grad: float32 [3, 4, 2048], replicated
Inputs may be any that keep to these rules, and one draw needn't show every extreme that they name: `block_lists`: entry n names key block n of the sequence. Each list names the 1 key block of its own query block and no block twice. The lists in the rows of ctx index i name only blocks held by ctx index i or by ctx indices (i - d) mod 64 for d = 1 to 6, and at most 2 distinct blocks held by any one other index; this most is reached.
All inputs are finite; a program needn't handle non-finite values.
Results may differ from a plain program's by a relative error of at most 0.012.
The roundings to bfloat16 on the way count: a program that leaves them out, or rounds other values in their place, can miss the bound.
Values may be sent and summed in bfloat16 or wider, within the bound.
No kernel may reach another device: no remote copies, remote signals or barrier semaphores. Data moves between devices by JAX's collectives and lax.ppermute only.
A program may use at most 192 MiB of HBM per device.

v0:
```python
import functools
import math

import jax
import jax.numpy as jnp
from jax import lax
from jax.experimental import pallas as pl
from jax.experimental.pallas import tpu as pltpu
from jax.sharding import PartitionSpec as P

HEAD = 128
TAPS = 4
BLK = 64
BEHIND = 6
MAX_REMOTE = 2
HALF = 128
OWN_BLOCKS = 4
PAD = 8
RUN = HALF + PAD
SLOTS = BEHIND * MAX_REMOTE
KEYS = SLOTS * BLK + 2 * HALF
GROUPS = 2
HIDDEN = 1 << 30
WIDE = 512
VMEM = 48 * 1024 * 1024


def along(x, pairs):
    return lax.ppermute(x, "ctx", pairs)


def ring_pairs(count, by):
    return [(i, (i + by) % count) for i in range(count)]


def sibling_pairs(count):
    return [(i, i ^ 1) for i in range(count)]


def wrapped_out(count, by):
    return [(i, i + by - count) for i in range(count - by, count)]


def wrapped_back(count, by):
    return [(j, i) for i, j in wrapped_out(count, by)]


def once(x, *others):
    return lax.optimization_barrier((x, others))[0]


def summed_over(x, axes, after):
    number = 0
    for axis in axes:
        count = lax.axis_size(axis)
        step = 1
        while step < count:
            x = once(x, *after.get(number, ()))
            x = x + lax.ppermute(x, axis, [(i, i ^ step) for i in range(count)])
            step *= 2
            number += 1
    return x


def shared(own, from_two, from_four, from_six, first_core, pairs):
    mine = jnp.stack(
        [
            jnp.where(first_core, own, from_two),
            jnp.where(first_core, from_two, from_four),
            jnp.where(first_core, from_four, from_six),
        ]
    )
    return along(mine, pairs)


def table_of_slots(lists, my_index, count):
    span = lists * BLK // HALF
    upper = span >= count
    owners = jnp.where(upper, 2 * count - 1 - span, span)
    local = jnp.where(upper, OWN_BLOCKS // 2, 0) + lists % (HALF // BLK)
    distance = ((my_index - owners) % count).reshape(-1)
    reach = BEHIND - jnp.arange(BEHIND, dtype=jnp.int32)
    block_ids = jnp.arange(OWN_BLOCKS, dtype=jnp.int32)
    wanted = jnp.any(
        (distance[:, None, None] == reach[None, :, None])
        & (local.reshape(-1)[:, None, None] == block_ids[None, None, :]),
        axis=0,
    )
    rank = jnp.cumsum(wanted.astype(jnp.int32), axis=1) - 1
    slot_ids = jnp.arange(MAX_REMOTE, dtype=jnp.int32)
    hits = wanted[:, :, None] & (rank[:, :, None] == slot_ids[None, None, :])
    chosen = jnp.sum(jnp.where(hits, block_ids[None, :, None], 0), axis=1)
    chosen_named = jnp.any(hits, axis=1)
    wraps = (reach > my_index)[:, None]
    block = jnp.where(wraps, chosen, slot_ids[None, :])
    named = jnp.where(wraps, chosen_named, wanted[:, :MAX_REMOTE])
    rows = jnp.arange(BEHIND, dtype=jnp.int32)[:, None]
    index = jnp.where(block < 2, rows * 2 + block, SLOTS + rows * 2 + block - 2)
    owner = ((my_index - reach) % count)[:, None]
    piece = jnp.where(block < 2, owner, 2 * count - 1 - owner)
    start = piece * HALF + (block % 2) * BLK
    start = jnp.where(named, start, HIDDEN)
    spread = jnp.arange(BLK, dtype=jnp.int32)
    positions = (start.reshape(-1)[:, None] + spread[None, :]).reshape(-1)
    return index.reshape(-1), positions


def attention_kernel(
    meta, key_pos, query_pos, q_raw, k_raw, v_raw, cot, weight, q_halo, far_halo, high_halo,
    two, four, six, odd, e_two, e_four, e_six, e_odd,
    dq_out, own_out, odd_out, even_out, e_odd_out, e_even_out, taps_out,
    hide, xq, xk, xv, kall, vall, kt, vt, scores, dprob, probs_half, dscore, gk, gv,
):
    my_index = meta[SLOTS]
    wrapping = my_index < BEHIND
    scale = HEAD ** -0.5
    f32 = jnp.float32
    half = jnp.bfloat16

    @pl.when(pl.program_id(0) == 0)
    def _():
        hide[...] = jnp.where(key_pos[...] <= query_pos[...], 0.0, -jnp.inf)
        gk[...] = jnp.zeros_like(gk)
        gv[...] = jnp.zeros_like(gv)

    raw = (xk, xv)
    fields = (kall, vall)
    tables = (kt, vt)
    near = {1: lambda n: odd[0, n], 3: lambda n: odd[1, n], 5: lambda n: odd[2, n],
            2: lambda n: two[n], 4: lambda n: four[n], 6: lambda n: six[n]}
    wrapped = {1: lambda n: e_odd[0, n], 3: lambda n: e_odd[1, n], 5: lambda n: e_odd[2, n],
               2: lambda n: e_two[n], 4: lambda n: e_four[n], 6: lambda n: e_six[n]}

    def convolved(x, place, which):
        base = place * RUN + PAD
        total = weight[which, 0:1, :] * x[base : base + HALF, :]
        for tap in range(1, TAPS):
            total = total + weight[which, tap : tap + 1, :] * x[base - tap : base - tap + HALF, :]
        return total.astype(half)

    def last_rows(x, place):
        return x[place * RUN + HALF : place * RUN + RUN, :]

    for side in range(2):
        xq[side * RUN : side * RUN + PAD, :] = q_halo[side]
        xq[side * RUN + PAD : (side + 1) * RUN, :] = q_raw[side * HALF : (side + 1) * HALF, :].astype(f32)
    queries = jnp.concatenate([convolved(xq, 0, 0), convolved(xq, 1, 0)], axis=0)

    own_raw = (k_raw, v_raw)
    for n in range(2):
        x = raw[n]
        for place in range(BEHIND + 1):
            base = place * RUN
            if place < BEHIND:
                rows = near[BEHIND - place](n).astype(f32)
            else:
                rows = own_raw[n][0:HALF, :].astype(f32)
            before = far_halo[n] if place == 0 else last_rows(x, place - 1)
            x[base : base + PAD, :] = jnp.where(BEHIND - place == my_index, 0.0, before)
            x[base + PAD : base + RUN, :] = rows
        base = (BEHIND + 1) * RUN
        x[base : base + PAD, :] = high_halo[n]
        x[base + PAD : base + RUN, :] = own_raw[n][HALF : 2 * HALF, :].astype(f32)
        for place in range(BEHIND):
            fields[n][place * HALF : (place + 1) * HALF, :] = convolved(x, place, n + 1)
        for side in range(2):
            first = SLOTS * BLK + side * HALF
            tables[n][first : first + HALF, :] = convolved(x, BEHIND + side, n + 1)

    @pl.when(wrapping)
    def _():
        gk[...] = jnp.zeros_like(gk)
        gv[...] = jnp.zeros_like(gv)
        for n in range(2):
            x = raw[n]
            for step in range(1, BEHIND + 1):
                place = BEHIND - step
                base = (BEHIND + 2 + place) * RUN
                before = last_rows(x, place)
                if step > 1:
                    before = jnp.where(step == my_index + 1, before, last_rows(x, BEHIND + 3 + place))
                x[base : base + PAD, :] = before
                x[base + PAD : base + RUN, :] = wrapped[step](n).astype(f32)
                first = (BEHIND + place) * HALF
                fields[n][first : first + HALF, :] = convolved(x, BEHIND + 2 + place, n + 1)

    for slot in range(SLOTS):
        source = pl.ds(pl.multiple_of(meta[slot] * BLK, BLK), BLK)
        for n in range(2):
            tables[n][slot * BLK : (slot + 1) * BLK, :] = fields[n][source, :]

    grads = cot[...]
    contract_last = (((1,), (1,)), ((), ()))
    contract_first = (((0,), (0,)), ((), ()))
    plain = (((1,), (0,)), ((), ()))
    chunk = 128
    chunks = [slice(c, c + chunk) for c in range(0, KEYS, chunk)]
    width = 2 * HALF

    def folded(x, op):
        return op(x.reshape(chunk // 8, 8, width), axis=0)

    factor = scale * math.log2(math.e)
    tops = None
    for c in chunks:
        s = lax.dot_general(kt[c, :], queries, contract_last, preferred_element_type=f32)
        s = s * factor + hide[c, :]
        scores[c, :] = s
        top = folded(s, jnp.max)
        tops = top if tops is None else jnp.maximum(tops, top)
    top = jnp.max(tops, axis=0, keepdims=True)
    totals = jnp.zeros((8, width), f32)
    for c in chunks:
        e = jnp.exp2(scores[c, :] - top)
        scores[c, :] = e
        totals = totals + folded(e, jnp.sum)
    inverse = 1.0 / jnp.sum(totals, axis=0, keepdims=True)
    deltas = jnp.zeros((8, width), f32)
    for c in chunks:
        p = scores[c, :] * inverse
        scores[c, :] = p
        pb = p.astype(half)
        probs_half[c, :] = pb
        dp = lax.dot_general(vt[c, :], grads, contract_last, preferred_element_type=f32)
        dprob[c, :] = dp
        deltas = deltas + folded(pb.astype(f32) * dp, jnp.sum)
    delta = jnp.sum(deltas, axis=0, keepdims=True)
    for number, c in enumerate(chunks):
        ds = (scores[c, :] * (dprob[c, :] - delta)).astype(half)
        dscore[c, :] = ds
        dk = lax.dot_general(ds, queries, plain, preferred_element_type=f32) * scale
        dv = lax.dot_general(probs_half[c, :], grads, plain, preferred_element_type=f32)
        for n, (out, term) in enumerate(((gk, dk), (gv, dv))):
            if c.start < SLOTS * BLK:
                for part in range(chunk // BLK):
                    slot = number * (chunk // BLK) + part
                    target = pl.ds(pl.multiple_of(meta[slot] * BLK, BLK), BLK)
                    out[target, :] = term[part * BLK : (part + 1) * BLK, :]
            else:
                first = c.start - SLOTS * BLK
                own_out[n, first : first + chunk, :] = term
    dq = lax.dot_general(dscore[...], kt[...], contract_first, preferred_element_type=f32) * scale
    dq_out[...] = dq

    def tap_sums(terms, x):
        sums = []
        for tap in range(TAPS):
            total = jnp.zeros((8, HEAD), f32)
            for rows, place in terms:
                base = place * RUN + PAD - tap
                total = total + jnp.sum((rows() * x[base : base + HALF, :]).reshape(HALF // 8, 8, HEAD), axis=0)
            sums.append(jnp.sum(total, axis=0, keepdims=True))
        return jnp.concatenate(sums, axis=0)

    taps_out[0] = tap_sums([(lambda s=s: dq_out[s * HALF : (s + 1) * HALF, :], s) for s in range(2)], xq)
    for n, g in enumerate((gk, gv)):
        terms = [(lambda p=p, g=g: g[p * HALF : (p + 1) * HALF, :], p) for p in range(BEHIND)]
        terms += [(lambda s=s, n=n: own_out[n, s * HALF : (s + 1) * HALF, :], BEHIND + s) for s in range(2)]
        taps_out[n + 1] = tap_sums(terms, raw[n])

    @pl.when(wrapping)
    def _():
        for n, g in enumerate((gk, gv)):
            terms = [
                (lambda p=p, g=g: g[(BEHIND + p) * HALF : (BEHIND + p + 1) * HALF, :], BEHIND + 2 + p)
                for p in range(BEHIND)
            ]
            taps_out[n + 1] = taps_out[n + 1] + tap_sums(terms, raw[n])

    for n, g in enumerate((gk, gv)):
        for step in range(1, BEHIND + 1):
            place = BEHIND - step
            low = g[place * HALF : (place + 1) * HALF, :]
            high = g[(BEHIND + place) * HALF : (BEHIND + place + 1) * HALF, :]
            if step % 2:
                odd_out[step // 2, n] = low.astype(half)
                e_odd_out[step // 2, n] = high.astype(half)
            else:
                even_out[step // 2 - 1, n] = low
                e_even_out[step // 2 - 1, n] = high


def attention_terms(group, heads, meta, key_pos, query_pos, tensors, weight, halos, near, wrapped):
    q_raw, k_raw, v_raw, cot = tensors
    first = group * heads
    smem = pl.BlockSpec(memory_space=pltpu.SMEM)

    def whole(shape):
        return pl.BlockSpec(shape, lambda h: (0,) * len(shape))

    def of_head(*lead):
        return pl.BlockSpec(lead + (HEAD,), lambda h: (0,) * len(lead) + (first + h,))

    def of_group(*lead):
        return pl.BlockSpec(lead + (HEAD,), lambda h: (0,) * len(lead) + (h,))

    rows = 2 * HALF
    channels = heads * HEAD
    f32 = jnp.float32
    half = jnp.bfloat16
    piece = of_group(2, HALF)
    pieces = of_group(3, 2, HALF)
    run = functools.partial(pltpu.VMEM)
    return pl.pallas_call(
        attention_kernel,
        grid=(heads,),
        in_specs=[
            smem, whole((KEYS, 1)), whole((1, rows)),
            of_head(rows), of_head(rows), of_head(rows), of_head(rows),
            of_head(3, TAPS), of_head(2, PAD), of_head(2, PAD), of_head(2, PAD),
            piece, piece, piece, pieces, piece, piece, piece, pieces,
        ],
        out_specs=[of_group(rows), of_group(2, rows), pieces, pieces, pieces, pieces, of_group(3, TAPS)],
        out_shape=[
            jax.ShapeDtypeStruct((rows, channels), f32),
            jax.ShapeDtypeStruct((2, rows, channels), f32),
            jax.ShapeDtypeStruct((3, 2, HALF, channels), half),
            jax.ShapeDtypeStruct((3, 2, HALF, channels), f32),
            jax.ShapeDtypeStruct((3, 2, HALF, channels), half),
            jax.ShapeDtypeStruct((3, 2, HALF, channels), f32),
            jax.ShapeDtypeStruct((3, TAPS, channels), f32),
        ],
        scratch_shapes=[
            run((KEYS, rows), f32),
            run((2 * RUN, HEAD), f32),
            run((14 * RUN, HEAD), f32), run((14 * RUN, HEAD), f32),
            run((2 * BEHIND * HALF, HEAD), half), run((2 * BEHIND * HALF, HEAD), half),
            run((KEYS, HEAD), half), run((KEYS, HEAD), half),
            run((KEYS, rows), f32), run((KEYS, rows), f32),
            run((KEYS, rows), half), run((KEYS, rows), half),
            run((2 * BEHIND * HALF, HEAD), f32), run((2 * BEHIND * HALF, HEAD), f32),
        ],
        compiler_params=pltpu.CompilerParams(vmem_limit_bytes=VMEM),
        cost_estimate=pl.CostEstimate(
            flops=heads * 100 * rows * KEYS * HEAD, bytes_accessed=heads * 3 * 1024 * 1024, transcendentals=heads * rows * KEYS
        ),
        name="attention",
    )(meta, key_pos, query_pos, q_raw, k_raw, v_raw, cot, weight, *halos, *near, *wrapped)


def unconvolved(rows, after, taps):
    extended = jnp.concatenate([rows, after], axis=0)
    total = taps[0:1, :] * extended[:HALF, :]
    for tap in range(1, TAPS):
        total = total + taps[tap : tap + 1, :] * extended[tap : tap + HALF, :]
    return total.astype(jnp.bfloat16)


def query_kernel(grad, after, weight, out):
    for side in range(2):
        rows = slice(side * HALF, (side + 1) * HALF)
        out[rows, :] = unconvolved(grad[rows, :], after[side], weight[0])


def final_kernel(terms, meta, own, beside, after, weight, *rest):
    outs = rest[-2:]
    sent = rest[:terms]
    e_sent = rest[terms : terms + 2]
    f32 = jnp.float32
    first_core = meta[0] % 2 == 0
    for n in range(2):
        low = own[n, 0:HALF, :] + jnp.where(first_core, beside[0, n].astype(f32), 0.0)
        for x in sent:
            low = low + x[n].astype(f32)
        high = own[n, HALF : 2 * HALF, :]
        for x in e_sent:
            high = high + x[n].astype(f32)
        outs[n][0:HALF, :] = unconvolved(low, after[n, 0], weight[n + 1])
        outs[n][HALF : 2 * HALF, :] = unconvolved(high, after[n, 1], weight[n + 1])


def combine_kernel(meta, even, odd, e_even, e_odd, two, four, six, e_two, e_four, e_six):
    f32 = jnp.float32
    first_core = meta[0] % 2 == 0
    for evens, odds, outs in ((even, odd, (two, four, six)), (e_even, e_odd, (e_two, e_four, e_six))):
        for n in range(2):
            wide = [odds[m, n].astype(f32) for m in range(3)]
            beside = [
                jnp.where(first_core, wide[1], wide[0]),
                jnp.where(first_core, wide[2], wide[1]),
                jnp.where(first_core, 0.0, wide[2]),
            ]
            for m, out in enumerate(outs):
                out[n] = (evens[m, n] + beside[m]).astype(out.dtype)


def combined(meta, even, odd, e_even, e_odd, six_type):
    channels = even.shape[-1]
    wide = min(WIDE, channels)
    half = jnp.bfloat16
    f32 = jnp.float32
    pieces = pl.BlockSpec((3, 2, HALF, wide), lambda h: (0, 0, 0, h))
    piece = pl.BlockSpec((2, HALF, wide), lambda h: (0, 0, h))
    types = [half, half, six_type, half, half, f32]
    return pl.pallas_call(
        combine_kernel,
        grid=(channels // wide,),
        in_specs=[pl.BlockSpec(memory_space=pltpu.SMEM)] + [pieces] * 4,
        out_specs=[piece] * 6,
        out_shape=[jax.ShapeDtypeStruct((2, HALF, channels), t) for t in types],
        compiler_params=pltpu.CompilerParams(vmem_limit_bytes=VMEM),
        name="combine",
    )(meta, even, odd, e_even, e_odd)


def finished(group, heads, meta, own, near, beside, wrapped, after, weight, earlier):
    rows = 2 * HALF
    channels = heads * HEAD
    wide = min(WIDE, channels)
    first = group * (channels // wide)

    def of_group(*lead):
        return pl.BlockSpec(lead + (wide,), lambda h: (0,) * len(lead) + (h,))

    def of_head(*lead):
        return pl.BlockSpec(lead + (wide,), lambda h: (0,) * len(lead) + (first + h,))

    piece = of_group(2, HALF)
    anywhere = pl.BlockSpec(memory_space=pl.ANY)
    shape = jax.ShapeDtypeStruct((rows, GROUPS * channels), jnp.bfloat16)
    extra = [] if earlier is None else list(earlier)
    terms = len(near) + len(wrapped)
    return pl.pallas_call(
        functools.partial(final_kernel, len(near)),
        grid=(channels // wide,),
        in_specs=[
            pl.BlockSpec(memory_space=pltpu.SMEM), of_group(2, rows), of_group(1, 2, HALF),
            of_head(2, 2, PAD), of_head(3, TAPS),
        ]
        + [piece] * terms
        + [anywhere] * len(extra),
        out_specs=[of_head(rows), of_head(rows)],
        out_shape=[shape, shape],
        input_output_aliases={5 + terms + n: n for n in range(len(extra))},
        compiler_params=pltpu.CompilerParams(vmem_limit_bytes=VMEM),
        name="finish",
    )(meta, own, beside, after, weight, *near, *wrapped, *extra)


def body(query_in, key_in, value_in, conv_weight, out_grad, block_lists):
    q_raw, k_raw, v_raw, cot = (x[0] for x in (query_in, key_in, value_in, out_grad))
    f32 = jnp.float32
    half = jnp.bfloat16
    channels = q_raw.shape[1]
    rows = 2 * HALF
    heads = channels // HEAD // GROUPS
    width = heads * HEAD
    count = lax.axis_size("ctx")
    my_index = lax.axis_index("ctx")
    first_core = my_index % 2 == 0
    is_last = my_index == count - 1
    up = [(i, i + 1) for i in range(count - 1)]
    down = [(i + 1, i) for i in range(count - 1)]
    every = sibling_pairs(count)
    few = sibling_pairs(BEHIND)

    tail = slice(HALF - PAD, HALF)
    high_tail = slice(rows - PAD, rows)
    q_before = along(q_raw[tail], up)
    far = along(jnp.stack([k_raw[tail], v_raw[tail]]), ring_pairs(count, BEHIND + 1))
    above = along(jnp.stack([x[high_tail] for x in (q_raw, k_raw, v_raw)]), down)

    near = []
    wrapped = []
    for group in range(GROUPS):
        part = slice(group * width, (group + 1) * width)
        low = jnp.stack([k_raw[:HALF, part], v_raw[:HALF, part]])
        high = jnp.stack([k_raw[HALF:, part], v_raw[HALF:, part]])
        if group:
            low, high = once((low, high), ready)
        two = along(low, ring_pairs(count, 2))
        six = along(low, ring_pairs(count, 6))
        if group == 0:
            ready = once(six, q_before, far, above)
            four = along(ready, ring_pairs(count, -2))
        else:
            four = along(low, ring_pairs(count, 4))
        e_two = along(high, wrapped_out(count, 2))
        e_six = along(high, wrapped_out(count, 6))
        e_four = along(e_six, [(i + 2, i) for i in range(4)])
        near.append((two, four, six, low))
        wrapped.append((e_two, e_four, e_six, high))

    below = jnp.stack([x[tail] for x in (q_raw, k_raw, v_raw)])
    above = jnp.where(is_last, below, above).astype(f32)
    q_halo = jnp.stack([q_before.astype(f32), above[0]])
    halos = (q_halo, far.astype(f32), above[1:])

    index, remote_pos = table_of_slots(block_lists[0], my_index, count)
    spread = jnp.arange(HALF, dtype=jnp.int32)
    positions = jnp.concatenate([my_index * HALF + spread, (2 * count - 1 - my_index) * HALF + spread])
    key_pos = jnp.concatenate([remote_pos, positions])[:, None]
    place = my_index[None].astype(jnp.int32)
    meta = jnp.concatenate([index, place]).astype(jnp.int32)

    results = []
    returned = []
    for group in range(GROUPS):
        two, four, six, low = near[group]
        e_two, e_four, e_six, high = wrapped[group]
        if group:
            low, high = once((low, high), results[-1][6])
        else:
            low, high = once((low, high), near[1][0])
        beside = shared(low, two, four, six, first_core, every)
        e_beside = shared(high, e_two, e_four, e_six, first_core, few)
        result = attention_terms(
            group, heads, meta, key_pos, positions[None, :], (q_raw, k_raw, v_raw, cot), conv_weight, halos,
            (two, four, six, beside), (e_two, e_four, e_six, e_beside),
        )
        _, _, odd, even, e_odd, e_even, _ = result
        if group:
            odd, e_odd = once((odd, e_odd), *returned[-1][0], returned[-1][2][0], e_merged)
        got = along(odd, every)
        e_got = along(e_odd, few)
        direct = group == 0
        two, four, six, e_two, e_four, e_six = combined(place, even, got, e_even, e_got, half if direct else f32)
        meta = once(meta, two)
        sent_two = along(two, ring_pairs(count, -2))
        if direct:
            sent_four = along(four, ring_pairs(count, -4))
        else:
            six = (six + along(four, ring_pairs(count, 2)).astype(f32)).astype(half)
        sent_six = along(six, ring_pairs(count, -6))
        e_sent_two = along(e_two, wrapped_back(count, 2))
        e_six = (e_six + along(e_four, [(i, i + 2) for i in range(4)]).astype(f32)).astype(half)
        e_merged = e_six
        e_sent_six = along(e_six, wrapped_back(count, 6))
        sent = (sent_two, sent_four, sent_six) if direct else (sent_two, sent_six)
        results.append(result)
        returned.append((sent, got, (e_sent_two, e_sent_six)))
        last_two = two

    kernel_terms = jnp.concatenate([r[6] for r in results], axis=2)
    first_sent = (returned[-1][0][0], returned[-1][2][0])
    kernel_grad = summed_over(kernel_terms, ("ctx", "dp"), {2: (last_two,), 4: first_sent})

    def after_rows(heads_of):
        low, high = heads_of
        next_low = along(low, down)
        next_high = along(high, up)
        return jnp.stack([jnp.where(is_last, high, next_low), next_high], axis=-3)

    dq = once(jnp.concatenate([r[0] for r in results], axis=1), *first_sent)
    q_after = after_rows((dq[:PAD], dq[HALF : HALF + PAD]))
    wide = min(WIDE, width)
    spec = pl.BlockSpec((rows, wide), lambda h: (0, h))
    query_grad = pl.pallas_call(
        query_kernel,
        grid=(channels // wide,),
        in_specs=[
            spec,
            pl.BlockSpec((2, PAD, wide), lambda h: (0, 0, h)),
            pl.BlockSpec((3, TAPS, wide), lambda h: (0, 0, h)),
        ],
        out_specs=spec,
        out_shape=jax.ShapeDtypeStruct((rows, channels), half),
        compiler_params=pltpu.CompilerParams(vmem_limit_bytes=VMEM),
        name="query_finish",
    )(dq, q_after, conv_weight)

    lows = []
    highs = []
    for group in range(GROUPS):
        own = results[group][1]
        sent, got, e_sent = returned[group]
        low = own[:, :PAD] + jnp.where(first_core, got[0, :, :PAD].astype(f32), 0.0)
        high = own[:, HALF : HALF + PAD]
        for x in sent:
            low = low + x[:, :PAD].astype(f32)
        for x in e_sent:
            high = high + x[:, :PAD].astype(f32)
        lows.append(low)
        highs.append(high)
    after = after_rows((jnp.concatenate(lows, axis=2), jnp.concatenate(highs, axis=2)))
    outs = None
    for group in range(GROUPS):
        sent, got, e_sent = returned[group]
        outs = finished(group, heads, place, results[group][1], sent, got, e_sent, after, conv_weight, outs)
    return (query_grad[None], outs[0][None], outs[1][None], kernel_grad)


def solution(mesh):
    placed = (
        P("dp", "ctx", None),
        P("dp", "ctx", None),
        P("dp", "ctx", None),
        P(),
        P("dp", "ctx", None),
        P("dp", "ctx", None),
    )
    return jax.shard_map(
        body,
        mesh=mesh,
        in_specs=placed,
        out_specs=(P("dp", "ctx", None), P("dp", "ctx", None), P("dp", "ctx", None), P()),
        check_vma=False,
    )
```

profile of v0, /device:TPU:8, one launch (start us, length us, event | category | flops | bytes accessed | tf_op | source)
XLA Modules:
  0.0 331.2 jit_solution(18184426064367470248)
XLA Ops:
  4.3 3.2 collective-permute-start.2
  11.6 3.0 collective-permute-start.4
  20.8 9.3 %collective-permute-done.4.six = bf16[2,128,1024]{2,1,0:T(8,128)(2,1)S(1)} collective-permute-done((bf16[2,128,1024]{2,1,0:T(8,128)(2,1)}, bf16[2,128,1024]{2,1,0:T(8,128)(2,1)S(1)}, u32[]{:S(2)}, u32[]{:S(2)}) %collective-permute-start.4) | collective-permute-done | bytes 524320 | tf_op jit(solution)/shard_map/ppermute | solution.py:29
  33.0 7.4 %collective-permute-done.9.e_six = bf16[2,128,1024]{2,1,0:T(8,128)(2,1)S(1)} collective-permute-done((bf16[2,128,1024]{2,1,0:T(8,128)(2,1)}, bf16[2,128,1024]{2,1,0:T(8,128)(2,1)S(1)}, u32[]{:S(2)}, u32[]{:S(2)}) %collective-permute-start.9) | collective-permute-done | bytes 524320 | tf_op jit(solution)/shard_map/ppermute | solution.py:29
  40.4 2.7 collective-permute-start.10
  45.2 6.5 %collective-permute-done.5.four = bf16[2,128,1024]{2,1,0:T(8,128)(2,1)} collective-permute-done((bf16[2,128,1024]{2,1,0:T(8,128)(2,1)S(1)}, bf16[2,128,1024]{2,1,0:T(8,128)(2,1)}, u32[]{:S(2)}, u32[]{:S(2)}) %collective-permute-start.5) | collective-permute-done | bytes 524320 | tf_op jit(solution)/shard_map/ppermute | solution.py:29
  54.4 8.5 %collective-permute-done.10.e_four = bf16[2,128,1024]{2,1,0:T(8,128)(2,1)} collective-permute-done((bf16[2,128,1024]{2,1,0:T(8,128)(2,1)S(1)}, bf16[2,128,1024]{2,1,0:T(8,128)(2,1)}, u32[]{:S(2)}, u32[]{:S(2)}) %collective-permute-start.10) | collective-permute-done | bytes 524320 | tf_op jit(solution)/shard_map/ppermute | solution.py:29
  70.8 16.8 %collective-permute-done.18.e_six = bf16[2,128,1024]{2,1,0:T(8,128)(2,1)S(1)} collective-permute-done((bf16[2,128,1024]{2,1,0:T(8,128)(2,1)}, bf16[2,128,1024]{2,1,0:T(8,128)(2,1)S(1)}, u32[]{:S(2)}, u32[]{:S(2)}) %collective-permute-start.18) | collective-permute-done | bytes 524320 | tf_op jit(solution)/shard_map/ppermute | solution.py:29
  87.6 18.0 %collective-permute-start.19 = (bf16[2,128,1024]{2,1,0:T(8,128)(2,1)S(1)}, bf16[2,128,1024]{2,1,0:T(8,128)(2,1)S(1)}, u32[]{:S(2)}, u32[]{:S(2)}) collective-permute-start(bf16[2,128,1024]{2,1,0:T(8,128)(2,1)S(1)} %collective-permute-done.18.e_six), channel_id=1, source_target_pairs={{2,0},{3,1},{4,2},{5,3},{66,64},{67,65},{68,66},{69,67},{130,128},... | collective-permute-start | bytes 1572872 | tf_op jit(solution)/shard_map/ppermute | solution.py:29
  106.7 24.6 %attention.2 = (f32[256,1024]{1,0:T(8,128)S(1)}, f32[2,256,1024]{2,1,0:T(8,128)}, bf16[3,2,128,1024]{3,2,1,0:T(8,128)(2,1)}, f32[3,2,128,1024]{3,2,1,0:T(8,128)}...) custom-call(s32[13]{0:T(128)S(1)} %pad_add_fusion.2.meta, ...), custom_call_target="tpu_custom_call" | custom-call | flops 26843545600 | bytes 25165824 | tf_op jit(solution)/shard_map/attention/pallas_call | solution.py:304
  132.6 2.1 collective-permute-start.20
  140.3 4.5 %collective-permute-done.13.e_odd = bf16[3,2,128,1024]{3,2,1,0:T(8,128)(2,1)S(1)} collective-permute-done((bf16[3,2,128,1024]{3,2,1,0:T(8,128)(2,1)S(1)}, bf16[3,2,128,1024]{3,2,1,0:T(8,128)(2,1)S(1)}, u32[]{:S(2)}, u32[]{:S(2)}) %collective-permute-start.13) | collective-permute-done | bytes 1572896 | tf_op jit(solution)/shard_map/ppermute | solution.py:29
  146.0 3.9 %combine.2 = (bf16[2,128,1024]{2,1,0:T(8,128)(2,1)S(1)}, bf16[2,128,1024]{2,1,0:T(8,128)(2,1)S(1)}, bf16[2,128,1024]{2,1,0:T(8,128)(2,1)S(1)}, bf16[2,128,1024]{...) custom-call(s32[1]{0:T(128)} %bitcast.meta, ...), custom_call_target="tpu_custom_call" | custom-call | tf_op jit(solution)/shard_map/combine/pallas_call | solution.py:395
  149.9 2.6 collective-permute-start.21
  153.1 3.4 %collective-permute-start.25 = (bf16[2,128,1024]{2,1,0:T(8,128)(2,1)S(1)}, bf16[2,128,1024]{2,1,0:T(8,128)(2,1)S(1)}, u32[]{:S(2)}, u32[]{:S(2)}) collective-permute-start(bf16[2,128,1024]{2,1,0:T(8,128)(2,1)S(1)} %get-tuple-element.70), channel_id=1, source_target_pairs={{0,2},{1,3},{2,4},{3,5},{64,66},{65,67},{66,68},{67,69},{128,130},... | collective-permute-start | bytes 1572872 | tf_op jit(solution)/shard_map/ppermute | solution.py:29
  156.6 24.9 %attention.3 = (f32[256,1024]{1,0:T(8,128)S(1)}, f32[2,256,1024]{2,1,0:T(8,128)}, bf16[3,2,128,1024]{3,2,1,0:T(8,128)(2,1)}, f32[3,2,128,1024]{3,2,1,0:T(8,128)}...) custom-call(s32[13]{0:T(128)S(1)} %pad_add_fusion.2.meta, ...), custom_call_target="tpu_custom_call" | custom-call | flops 26843545600 | bytes 25165824 | tf_op jit(solution)/shard_map/attention/pallas_call | solution.py:304
  181.5 7.5 %collective-permute-done.25 = bf16[2,128,1024]{2,1,0:T(8,128)(2,1)S(1)} collective-permute-done((bf16[2,128,1024]{2,1,0:T(8,128)(2,1)S(1)}, bf16[2,128,1024]{2,1,0:T(8,128)(2,1)S(1)}, u32[]{:S(2)}, u32[]{:S(2)}) %collective-permute-start.25) | collective-permute-done | bytes 524320 | tf_op jit(solution)/shard_map/ppermute | solution.py:29
  191.0 2.4 collective-permute-start.27
  197.9 3.8 %combine.3 = (bf16[2,128,1024]{2,1,0:T(8,128)(2,1)S(1)}, bf16[2,128,1024]{2,1,0:T(8,128)(2,1)S(1)}, f32[2,128,1024]{2,1,0:T(8,128)S(1)}, bf16[2,128,1024]{2,1,0:...) custom-call(s32[1]{0:T(128)} %bitcast.meta, ...), custom_call_target="tpu_custom_call" | custom-call | tf_op jit(solution)/shard_map/combine/pallas_call | solution.py:395
  201.7 2.4 collective-permute-start.33
  205.7 21.9 %collective-permute-start.40 = (f32[3,4,2048]{2,1,0:T(4,128)S(1)}, f32[3,4,2048]{2,1,0:T(4,128)S(1)}, u32[]{:S(2)}, u32[]{:S(2)}) collective-permute-start(f32[3,4,2048]{2,1,0:T(4,128)S(1)} %add.227), channel_id=1, source_target_pairs={{0,2},{1,3},{2,0},{3,1},{4,6},{5,7},{6,4},{7,5},{8,10},{9,11},{10,... | collective-permute-start | bytes 294920 | tf_op jit(solution)/shard_map/ppermute | solution.py:59
  227.6 24.0 %collective-permute-done.40 = f32[3,4,2048]{2,1,0:T(4,128)S(1)} collective-permute-done((f32[3,4,2048]{2,1,0:T(4,128)S(1)}, f32[3,4,2048]{2,1,0:T(4,128)S(1)}, u32[]{:S(2)}, u32[]{:S(2)}) %collective-permute-start.40) | collective-permute-done | bytes 98336 | tf_op jit(solution)/shard_map/ppermute | solution.py:59
  253.3 5.6 %collective-permute-done.41 = f32[3,4,2048]{2,1,0:T(4,128)S(1)} collective-permute-done((f32[3,4,2048]{2,1,0:T(4,128)S(1)}, f32[3,4,2048]{2,1,0:T(4,128)S(1)}, u32[]{:S(2)}, u32[]{:S(2)}) %collective-permute-start.41) | collective-permute-done | bytes 98336 | tf_op jit(solution)/shard_map/ppermute | solution.py:59
  261.4 4.1 %collective-permute-done.42 = f32[3,4,2048]{2,1,0:T(4,128)S(1)} collective-permute-done((f32[3,4,2048]{2,1,0:T(4,128)S(1)}, f32[3,4,2048]{2,1,0:T(4,128)S(1)}, u32[]{:S(2)}, u32[]{:S(2)}) %collective-permute-start.42) | collective-permute-done | bytes 98336 | tf_op jit(solution)/shard_map/ppermute | solution.py:59
  265.5 3.3 collective-permute-done.28.rest_0_
  268.9 11.5 %collective-permute-done.43 = f32[3,4,2048]{2,1,0:T(4,128)S(1)} collective-permute-done((f32[3,4,2048]{2,1,0:T(4,128)S(1)}, f32[3,4,2048]{2,1,0:T(4,128)S(1)}, u32[]{:S(2)}, u32[]{:S(2)}) %collective-permute-start.43) | collective-permute-done | bytes 98336 | tf_op jit(solution)/shard_map/ppermute | solution.py:59
  281.5 15.3 %collective-permute-start.30 = (f32[8,2048]{1,0:T(8,128)S(1)}, f32[8,2048]{1,0:T(8,128)S(1)}, u32[]{:S(2)}, u32[]{:S(2)}) collective-permute-start(f32[8,2048]{1,0:T(8,128)S(1)} %slice.132), channel_id=1, source_target_pairs={{1,0},{2,1},{3,2},{4,3},{5,4},{6,5},{7,6},{8,7},{9,8},{10,9},{11,1... | collective-permute-start | bytes 196616 | tf_op jit(solution)/shard_map/ppermute | solution.py:29
  298.4 15.4 %collective-permute-start.37 = (f32[2,8,2048]{2,1,0:T(8,128)S(1)}, f32[2,8,2048]{2,1,0:T(8,128)S(1)}, u32[]{:S(2)}, u32[]{:S(2)}) collective-permute-start(f32[2,8,2048]{2,1,0:T(8,128)S(1)} %pad_maximum_fusion.13), channel_id=1, source_target_pairs={{1,0},{2,1},{3,2},{4,3},{5,4},{6,5},{7,6},{8,7},{9,8},{10,9},{11,1... | collective-permute-start | bytes 393224 | tf_op jit(solution)/shard_map/ppermute | solution.py:29
  315.8 3.1 collective-permute-start.46
  320.9 2.3 query_finish.1
  325.2 3.5 %finish.2 = (bf16[256,2048]{1,0:T(8,128)(2,1)}, bf16[256,2048]{1,0:T(8,128)(2,1)}) custom-call(s32[1]{0:T(128)} %bitcast.meta, f32[2,256,1024]{2,1,0:T(8,128)} %get-tuple-element.78.own, bf16[3,2,128,1024]{3,2,1,0:T(8,128)(2,1)S(1)} %collective-permute-done.12.odd.beside, f32[2,2,8,2048]{3,2,1,0:T(8,128)S(1)} %copy.25.after, f32[3,4,2048]{2,1,0:T(4,128)S(1)} %copy-done.1, ...), custom_call_target="tpu_custom_call" | custom-call | tf_op jit(solution)/shard_map/finish/pallas_call | solution.py:423
  328.7 2.5 finish.3
  (171 shorter events, 59.8 us)
Async XLA Ops:
  1.6 18.2 %collective-permute-start = (bf16[8,2048]{1,0:T(8,128)(2,1)S(1)}, bf16[8,2048]{1,0:T(8,128)(2,1)S(1)}, u32[]{:S(2)}, u32[]{:S(2)}) collective-permute-start(bf16[8,2048]{1,0:T(8,128)(2,1)S(1)} %get-tuple-element.106), channel_id=1, source_target_pairs={{0,1},{1,2},{2,3},{3,4},{4,5},{5,6},{6,7},{7,8},{8,9},{9,10},{10,1... | collective-permute-start | bytes 98312 | tf_op jit(solution)/shard_map/ppermute | solution.py:29
  4.3 15.8 %collective-permute-start.2 = (bf16[2,8,2048]{2,1,0:T(8,128)(2,1)S(1)}, bf16[2,8,2048]{2,1,0:T(8,128)(2,1)S(1)}, u32[]{:S(2)}, u32[]{:S(2)}) collective-permute-start(bf16[2,8,2048]{2,1,0:T(8,128)(2,1)S(1)} %pad_maximum_fusion.16), channel_id=1, source_target_pairs={{0,7},{1,8},{2,9},{3,10},{4,11},{5,12},{6,13},{7,14},{8,15},{9,16}... | collective-permute-start | bytes 196616 | tf_op jit(solution)/shard_map/ppermute | solution.py:29
  11.6 18.5 %collective-permute-start.4 = (bf16[2,128,1024]{2,1,0:T(8,128)(2,1)}, bf16[2,128,1024]{2,1,0:T(8,128)(2,1)S(1)}, u32[]{:S(2)}, u32[]{:S(2)}) collective-permute-start(bf16[2,128,1024]{2,1,0:T(8,128)(2,1)} %pad_maximum_fusion.5), channel_id=1, source_target_pairs={{0,6},{1,7},{2,8},{3,9},{4,10},{5,11},{6,12},{7,13},{8,14},{9,15},... | collective-permute-start | bytes 1572872 | tf_op jit(solution)/shard_map/ppermute | solution.py:29
  15.4 25.0 %collective-permute-start.9 = (bf16[2,128,1024]{2,1,0:T(8,128)(2,1)}, bf16[2,128,1024]{2,1,0:T(8,128)(2,1)S(1)}, u32[]{:S(2)}, u32[]{:S(2)}) collective-permute-start(bf16[2,128,1024]{2,1,0:T(8,128)(2,1)} %pad_maximum_fusion.6), channel_id=1, source_target_pairs={{58,0},{59,1},{60,2},{61,3},{62,4},{63,5},{122,64},{123,65},{124,6... | collective-permute-start | bytes 1572872 | tf_op jit(solution)/shard_map/ppermute | solution.py:29
  19.7 25.5 %collective-permute-start.3 = (bf16[2,128,1024]{2,1,0:T(8,128)(2,1)}, bf16[2,128,1024]{2,1,0:T(8,128)(2,1)S(1)}, u32[]{:S(2)}, u32[]{:S(2)}) collective-permute-start(bf16[2,128,1024]{2,1,0:T(8,128)(2,1)} %pad_maximum_fusion.5), channel_id=1, source_target_pairs={{0,2},{1,3},{2,4},{3,5},{4,6},{5,7},{6,8},{7,9},{8,10},{9,11},{10,... | collective-permute-start | bytes 1572872 | tf_op jit(solution)/shard_map/ppermute | solution.py:29
  20.1 34.4 %collective-permute-start.8 = (bf16[2,128,1024]{2,1,0:T(8,128)(2,1)}, bf16[2,128,1024]{2,1,0:T(8,128)(2,1)S(1)}, u32[]{:S(2)}, u32[]{:S(2)}) collective-permute-start(bf16[2,128,1024]{2,1,0:T(8,128)(2,1)} %pad_maximum_fusion.6), channel_id=1, source_target_pairs={{62,0},{63,1},{126,64},{127,65},{190,128},{191,129},{254,192},{255... | collective-permute-start | bytes 1572872 | tf_op jit(solution)/shard_map/ppermute | solution.py:29
  30.1 21.6 %collective-permute-start.5 = (bf16[2,128,1024]{2,1,0:T(8,128)(2,1)S(1)}, bf16[2,128,1024]{2,1,0:T(8,128)(2,1)}, u32[]{:S(2)}, u32[]{:S(2)}) collective-permute-start(bf16[2,128,1024]{2,1,0:T(8,128)(2,1)S(1)} %collective-permute-done.4.six), channel_id=1, source_target_pairs={{0,62},{1,63},{2,0},{3,1},{4,2},{5,3},{6,4},{7,5},{8,6},{9,7},{10,... | collective-permute-start | bytes 1572872 | tf_op jit(solution)/shard_map/ppermute | solution.py:29
  40.4 22.5 %collective-permute-start.10 = (bf16[2,128,1024]{2,1,0:T(8,128)(2,1)S(1)}, bf16[2,128,1024]{2,1,0:T(8,128)(2,1)}, u32[]{:S(2)}, u32[]{:S(2)}) collective-permute-start(bf16[2,128,1024]{2,1,0:T(8,128)(2,1)S(1)} %collective-permute-done.9.e_six), channel_id=1, source_target_pairs={{2,0},{3,1},{4,2},{5,3},{66,64},{67,65},{68,66},{69,67},{130,128},... | collective-permute-start | bytes 1572872 | tf_op jit(solution)/shard_map/ppermute | solution.py:29
  54.4 33.1 %collective-permute-start.7 = (bf16[3,2,128,1024]{3,2,1,0:T(8,128)(2,1)}, bf16[3,2,128,1024]{3,2,1,0:T(8,128)(2,1)}, u32[]{:S(2)}, u32[]{:S(2)}) collective-permute-start(bf16[3,2,128,1024]{3,2,1,0:T(8,128)(2,1)} %pad_maximum_fusion.1), channel_id=1, source_target_pairs={{0,1},{1,0},{2,3},{3,2},{4,5},{5,4},{6,7},{7,6},{8,9},{9,8},{10,11... | collective-permute-start | bytes 4718600 | tf_op jit(solution)/shard_map/ppermute | solution.py:29
  65.6 40.0 %collective-permute-start.11 = (bf16[3,2,128,1024]{3,2,1,0:T(8,128)(2,1)}, bf16[3,2,128,1024]{3,2,1,0:T(8,128)(2,1)}, u32[]{:S(2)}, u32[]{:S(2)}) collective-permute-start(bf16[3,2,128,1024]{3,2,1,0:T(8,128)(2,1)} %pad_maximum_fusion.2), channel_id=1, source_target_pairs={{0,1},{1,0},{2,3},{3,2},{4,5},{5,4},{64,65},{65,64},{66,67},{67,66... | collective-permute-start | bytes 4718600 | tf_op jit(solution)/shard_map/ppermute | solution.py:29
  68.6 18.9 %collective-permute-start.18 = (bf16[2,128,1024]{2,1,0:T(8,128)(2,1)}, bf16[2,128,1024]{2,1,0:T(8,128)(2,1)S(1)}, u32[]{:S(2)}, u32[]{:S(2)}) collective-permute-start(bf16[2,128,1024]{2,1,0:T(8,128)(2,1)} %get-tuple-element.61), channel_id=1, source_target_pairs={{58,0},{59,1},{60,2},{61,3},{62,4},{63,5},{122,64},{123,65},{124,6... | collective-permute-start | bytes 1572872 | tf_op jit(solution)/shard_map/ppermute | solution.py:29
  70.0 61.3 %collective-permute-start.17 = (bf16[2,128,1024]{2,1,0:T(8,128)(2,1)}, bf16[2,128,1024]{2,1,0:T(8,128)(2,1)S(1)}, u32[]{:S(2)}, u32[]{:S(2)}) collective-permute-start(bf16[2,128,1024]{2,1,0:T(8,128)(2,1)} %get-tuple-element.61), channel_id=1, source_target_pairs={{62,0},{63,1},{126,64},{127,65},{190,128},{191,129},{254,192},{255... | collective-permute-start | bytes 1572872 | tf_op jit(solution)/shard_map/ppermute | solution.py:29
  70.7 66.7 %collective-permute-start.15 = (bf16[2,128,1024]{2,1,0:T(8,128)(2,1)S(1)}, bf16[2,128,1024]{2,1,0:T(8,128)(2,1)S(1)}, u32[]{:S(2)}, u32[]{:S(2)}) collective-permute-start(bf16[2,128,1024]{2,1,0:T(8,128)(2,1)S(1)} %get-tuple-element.60), channel_id=1, source_target_pairs={{0,6},{1,7},{2,8},{3,9},{4,10},{5,11},{6,12},{7,13},{8,14},{9,15},... | collective-permute-start | bytes 1572872 | tf_op jit(solution)/shard_map/ppermute | solution.py:29
  87.6 49.8 %collective-permute-start.14 = (bf16[2,128,1024]{2,1,0:T(8,128)(2,1)S(1)}, bf16[2,128,1024]{2,1,0:T(8,128)(2,1)S(1)}, u32[]{:S(2)}, u32[]{:S(2)}) collective-permute-start(bf16[2,128,1024]{2,1,0:T(8,128)(2,1)S(1)} %get-tuple-element.60), channel_id=1, source_target_pairs={{0,4},{1,5},{2,6},{3,7},{4,8},{5,9},{6,10},{7,11},{8,12},{9,13},{1... | collective-permute-start | bytes 1572872 | tf_op jit(solution)/shard_map/ppermute | solution.py:29
  87.6 44.7 %collective-permute-start.19 = (bf16[2,128,1024]{2,1,0:T(8,128)(2,1)S(1)}, bf16[2,128,1024]{2,1,0:T(8,128)(2,1)S(1)}, u32[]{:S(2)}, u32[]{:S(2)}) collective-permute-start(bf16[2,128,1024]{2,1,0:T(8,128)(2,1)S(1)} %collective-permute-done.18.e_six), channel_id=1, source_target_pairs={{2,0},{3,1},{4,2},{5,3},{66,64},{67,65},{68,66},{69,67},{130,128},... | collective-permute-start | bytes 1572872 | tf_op jit(solution)/shard_map/ppermute | solution.py:29
  132.6 19.8 %collective-permute-start.20 = (bf16[3,2,128,1024]{3,2,1,0:T(8,128)(2,1)S(1)}, bf16[3,2,128,1024]{3,2,1,0:T(8,128)(2,1)}, u32[]{:S(2)}, u32[]{:S(2)}) collective-permute-start(bf16[3,2,128,1024]{3,2,1,0:T(8,128)(2,1)S(1)} %pad_maximum_fusion.4), channel_id=1, source_target_pairs={{0,1},{1,0},{2,3},{3,2},{4,5},{5,4},{64,65},{65,64},{66,67},{67,66... | collective-permute-start | bytes 4718600 | tf_op jit(solution)/shard_map/ppermute | solution.py:29
  149.9 41.2 %collective-permute-start.21 = (bf16[2,128,1024]{2,1,0:T(8,128)(2,1)S(1)}, bf16[2,128,1024]{2,1,0:T(8,128)(2,1)S(1)}, u32[]{:S(2)}, u32[]{:S(2)}) collective-permute-start(bf16[2,128,1024]{2,1,0:T(8,128)(2,1)S(1)} %get-tuple-element.56), channel_id=1, source_target_pairs={{0,62},{1,63},{2,0},{3,1},{4,2},{5,3},{6,4},{7,5},{8,6},{9,7},{10,... | collective-permute-start | bytes 1572872 | tf_op jit(solution)/shard_map/ppermute | solution.py:29
  152.4 37.6 %collective-permute-start.22 = (bf16[2,128,1024]{2,1,0:T(8,128)(2,1)S(1)}, bf16[2,128,1024]{2,1,0:T(8,128)(2,1)S(1)}, u32[]{:S(2)}, u32[]{:S(2)}) collective-permute-start(bf16[2,128,1024]{2,1,0:T(8,128)(2,1)S(1)} %get-tuple-element.66), channel_id=1, source_target_pairs={{0,60},{1,61},{2,62},{3,63},{4,0},{5,1},{6,2},{7,3},{8,4},{9,5},{1... | collective-permute-start | bytes 1572872 | tf_op jit(solution)/shard_map/ppermute | solution.py:29
  152.4 38.6 %collective-permute-start.23 = (bf16[2,128,1024]{2,1,0:T(8,128)(2,1)S(1)}, bf16[2,128,1024]{2,1,0:T(8,128)(2,1)S(1)}, u32[]{:S(2)}, u32[]{:S(2)}) collective-permute-start(bf16[2,128,1024]{2,1,0:T(8,128)(2,1)S(1)} %get-tuple-element.67), channel_id=1, source_target_pairs={{0,58},{1,59},{2,60},{3,61},{4,62},{5,63},{6,0},{7,1},{8,2},{9,3},... | collective-permute-start | bytes 1572872 | tf_op jit(solution)/shard_map/ppermute | solution.py:29
  152.4 38.6 %collective-permute-start.24 = (bf16[2,128,1024]{2,1,0:T(8,128)(2,1)S(1)}, bf16[2,128,1024]{2,1,0:T(8,128)(2,1)S(1)}, u32[]{:S(2)}, u32[]{:S(2)}) collective-permute-start(bf16[2,128,1024]{2,1,0:T(8,128)(2,1)S(1)} %get-tuple-element.68), channel_id=1, source_target_pairs={{0,62},{1,63},{64,126},{65,127},{128,190},{129,191},{192,254},{193... | collective-permute-start | bytes 1572872 | tf_op jit(solution)/shard_map/ppermute | solution.py:29
  153.1 35.9 %collective-permute-start.25 = (bf16[2,128,1024]{2,1,0:T(8,128)(2,1)S(1)}, bf16[2,128,1024]{2,1,0:T(8,128)(2,1)S(1)}, u32[]{:S(2)}, u32[]{:S(2)}) collective-permute-start(bf16[2,128,1024]{2,1,0:T(8,128)(2,1)S(1)} %get-tuple-element.70), channel_id=1, source_target_pairs={{0,2},{1,3},{2,4},{3,5},{64,66},{65,67},{66,68},{67,69},{128,130},... | collective-permute-start | bytes 1572872 | tf_op jit(solution)/shard_map/ppermute | solution.py:29
  201.7 57.9 %collective-permute-start.33 = (bf16[2,128,1024]{2,1,0:T(8,128)(2,1)S(1)}, bf16[2,128,1024]{2,1,0:T(8,128)(2,1)S(1)}, u32[]{:S(2)}, u32[]{:S(2)}) collective-permute-start(bf16[2,128,1024]{2,1,0:T(8,128)(2,1)S(1)} %get-tuple-element.80), channel_id=1, source_target_pairs={{0,2},{1,3},{2,4},{3,5},{64,66},{65,67},{66,68},{67,69},{128,130},... | collective-permute-start | bytes 1572872 | tf_op jit(solution)/shard_map/ppermute | solution.py:29
  204.3 55.5 %collective-permute-start.35 = (bf16[2,128,1024]{2,1,0:T(8,128)(2,1)S(1)}, bf16[2,128,1024]{2,1,0:T(8,128)(2,1)S(1)}, u32[]{:S(2)}, u32[]{:S(2)}) collective-permute-start(bf16[2,128,1024]{2,1,0:T(8,128)(2,1)S(1)} %get-tuple-element.82), channel_id=1, source_target_pairs={{0,2},{1,3},{2,4},{3,5},{4,6},{5,7},{6,8},{7,9},{8,10},{9,11},{10,... | collective-permute-start | bytes 1572872 | tf_op jit(solution)/shard_map/ppermute | solution.py:29
  205.7 45.9 %collective-permute-start.40 = (f32[3,4,2048]{2,1,0:T(4,128)S(1)}, f32[3,4,2048]{2,1,0:T(4,128)S(1)}, u32[]{:S(2)}, u32[]{:S(2)}) collective-permute-start(f32[3,4,2048]{2,1,0:T(4,128)S(1)} %add.227), channel_id=1, source_target_pairs={{0,2},{1,3},{2,0},{3,1},{4,6},{5,7},{6,4},{7,5},{8,10},{9,11},{10,... | collective-permute-start | bytes 294920 | tf_op jit(solution)/shard_map/ppermute | solution.py:59
  251.7 28.9 %collective-permute-start.32 = (bf16[2,128,1024]{2,1,0:T(8,128)(2,1)}, bf16[2,128,1024]{2,1,0:T(8,128)(2,1)S(1)}, u32[]{:S(2)}, u32[]{:S(2)}) collective-permute-start(bf16[2,128,1024]{2,1,0:T(8,128)(2,1)} %add_convert_fusion.2), channel_id=1, source_target_pairs={{0,58},{1,59},{2,60},{3,61},{4,62},{5,63},{64,122},{65,123},{66,12... | collective-permute-start | bytes 1572872 | tf_op jit(solution)/shard_map/ppermute | solution.py:29
  253.0 15.7 %collective-permute-start.28 = (bf16[2,128,1024]{2,1,0:T(8,128)(2,1)S(1)}, bf16[2,128,1024]{2,1,0:T(8,128)(2,1)S(1)}, u32[]{:S(2)}, u32[]{:S(2)}) collective-permute-start(bf16[2,128,1024]{2,1,0:T(8,128)(2,1)S(1)} %get-tuple-element.74), channel_id=1, source_target_pairs={{0,62},{1,63},{2,0},{3,1},{4,2},{5,3},{6,4},{7,5},{8,6},{9,7},{10,... | collective-permute-start | bytes 1572872 | tf_op jit(solution)/shard_map/ppermute | solution.py:29
  259.9 38.4 %collective-permute-start.34 = (bf16[2,128,1024]{2,1,0:T(8,128)(2,1)S(1)}, bf16[2,128,1024]{2,1,0:T(8,128)(2,1)S(1)}, u32[]{:S(2)}, u32[]{:S(2)}) collective-permute-start(bf16[2,128,1024]{2,1,0:T(8,128)(2,1)S(1)} %add_convert_fusion.1), channel_id=1, source_target_pairs={{0,58},{1,59},{2,60},{3,61},{4,62},{5,63},{64,122},{65,123},{66,12... | collective-permute-start | bytes 1572872 | tf_op jit(solution)/shard_map/ppermute | solution.py:29
  265.4 32.9 %collective-permute-start.36 = (bf16[2,128,1024]{2,1,0:T(8,128)(2,1)S(1)}, bf16[2,128,1024]{2,1,0:T(8,128)(2,1)S(1)}, u32[]{:S(2)}, u32[]{:S(2)}) collective-permute-start(bf16[2,128,1024]{2,1,0:T(8,128)(2,1)S(1)} %add_convert_fusion), channel_id=1, source_target_pairs={{0,58},{1,59},{2,60},{3,61},{4,62},{5,63},{6,0},{7,1},{8,2},{9,3},... | collective-permute-start | bytes 1572872 | tf_op jit(solution)/shard_map/ppermute | solution.py:29
  280.4 16.3 %collective-permute-start.44 = (f32[3,4,2048]{2,1,0:T(4,128)S(1)}, f32[3,4,2048]{2,1,0:T(4,128)S(1)}, u32[]{:S(2)}, u32[]{:S(2)}) collective-permute-start(f32[3,4,2048]{2,1,0:T(4,128)S(1)} %add.231), channel_id=1, source_target_pairs={{0,32},{1,33},{2,34},{3,35},{4,36},{5,37},{6,38},{7,39},{8,40},{9,... | collective-permute-start | bytes 294920 | tf_op jit(solution)/shard_map/ppermute | solution.py:59
  281.5 32.3 %collective-permute-start.30 = (f32[8,2048]{1,0:T(8,128)S(1)}, f32[8,2048]{1,0:T(8,128)S(1)}, u32[]{:S(2)}, u32[]{:S(2)}) collective-permute-start(f32[8,2048]{1,0:T(8,128)S(1)} %slice.132), channel_id=1, source_target_pairs={{1,0},{2,1},{3,2},{4,3},{5,4},{6,5},{7,6},{8,7},{9,8},{10,9},{11,1... | collective-permute-start | bytes 196616 | tf_op jit(solution)/shard_map/ppermute | solution.py:29
  296.8 18.9 %collective-permute-start.45 = (f32[3,4,2048]{2,1,0:T(4,128)S(1)}, f32[3,4,2048]{2,1,0:T(4,128)S(1)}, u32[]{:S(2)}, u32[]{:S(2)}) collective-permute-start(f32[3,4,2048]{2,1,0:T(4,128)S(1)} %add.232), channel_id=1, source_target_pairs={{0,64},{64,0},{128,192},{192,128},{1,65},{65,1},{129,193},{193,129... | collective-permute-start | bytes 294920 | tf_op jit(solution)/shard_map/ppermute | solution.py:59
  298.4 20.5 %collective-permute-start.37 = (f32[2,8,2048]{2,1,0:T(8,128)S(1)}, f32[2,8,2048]{2,1,0:T(8,128)S(1)}, u32[]{:S(2)}, u32[]{:S(2)}) collective-permute-start(f32[2,8,2048]{2,1,0:T(8,128)S(1)} %pad_maximum_fusion.13), channel_id=1, source_target_pairs={{1,0},{2,1},{3,2},{4,3},{5,4},{6,5},{7,6},{8,7},{9,8},{10,9},{11,1... | collective-permute-start | bytes 393224 | tf_op jit(solution)/shard_map/ppermute | solution.py:29
  (29 other events, 362.1 us)
where the time goes:
time: 334 us; the launch traced here: 331 us
  starting transfers between devices  121 us (36%)
  waiting for transfers between devices  119 us (36%)
  Pallas kernels  65.6 us (20%)
  other arithmetic  16.2 us (5%)
  local copies, waits for them, and re-layouts  7.98 us (2%)
    ppermute x39, starting transfers between devices, along(): return lax.ppermute(x, 'ctx', pairs)  94.2 us
    ppermute x39, waiting for transfers between devices, along(): return lax.ppermute(x, 'ctx', pairs)  72.7 us
    pallas_call x2, Pallas kernels, attention_terms(): pl.pallas_call(attention_kernel, grid=(heads,), in_specs=[smem, whole((KE...  49.6 us
    ppermute x8, waiting for transfers between devices, summed_over(): x = x + lax.ppermute(x, axis, [(i, i ^ step) for i in range(count)])  46.3 us
    ppermute x8, starting transfers between devices, summed_over(): x = x + lax.ppermute(x, axis, [(i, i ^ step) for i in range(count)])  26.9 us
    pallas_call x2, Pallas kernels, combined(): pl.pallas_call(combine_kernel, grid=(channels // wide,), in_specs=[pl.Blo...  7.72 us
    another operation x8, other arithmetic, shared(): jnp.stack([jnp.where(first_core, own, from_two), jnp.where(first_core, fr...  7.07 us
  transfers between devices with their start and end apart: 47, of which 20 were waited for; matrix products, arithmetic and copies ran while one was open for 6% of the time, Pallas kernels for 17%

commit v1 on v0

--- a/solution.py
+++ b/solution.py
@@ -49,16 +49,19 @@
     return lax.optimization_barrier((x, others))[0]
 
 
-def summed_over(x, axes, after):
-    number = 0
+def exchange_steps(axes):
+    steps = []
     for axis in axes:
-        count = lax.axis_size(axis)
         step = 1
-        while step < count:
-            x = once(x, *after.get(number, ()))
-            x = x + lax.ppermute(x, axis, [(i, i ^ step) for i in range(count)])
+        while step < lax.axis_size(axis):
+            steps.append((axis, step))
             step *= 2
-            number += 1
+    return steps
+
+
+def exchanged(x, steps):
+    for axis, step in steps:
+        x = x + lax.ppermute(x, axis, [(i, i ^ step) for i in range(lax.axis_size(axis))])
     return x
 
 
@@ -384,14 +387,14 @@
                 out[n] = (evens[m, n] + beside[m]).astype(out.dtype)
 
 
-def combined(meta, even, odd, e_even, e_odd, six_type):
+def combined(meta, even, odd, e_even, e_odd):
     channels = even.shape[-1]
     wide = min(WIDE, channels)
     half = jnp.bfloat16
     f32 = jnp.float32
     pieces = pl.BlockSpec((3, 2, HALF, wide), lambda h: (0, 0, 0, h))
     piece = pl.BlockSpec((2, HALF, wide), lambda h: (0, 0, h))
-    types = [half, half, six_type, half, half, f32]
+    types = [half] * 5 + [f32]
     return pl.pallas_call(
         combine_kernel,
         grid=(channels // wide,),
@@ -477,9 +480,8 @@
             four = along(low, ring_pairs(count, 4))
         e_two = along(high, wrapped_out(count, 2))
         e_six = along(high, wrapped_out(count, 6))
-        e_four = along(e_six, [(i + 2, i) for i in range(4)])
         near.append((two, four, six, low))
-        wrapped.append((e_two, e_four, e_six, high))
+        wrapped.append((e_two, e_six, high))
 
     below = jnp.stack([x[tail] for x in (q_raw, k_raw, v_raw)])
     above = jnp.where(is_last, below, above).astype(f32)
@@ -493,15 +495,17 @@
     place = my_index[None].astype(jnp.int32)
     meta = jnp.concatenate([index, place]).astype(jnp.int32)
 
+    steps = exchange_steps(("ctx", "dp"))
     results = []
     returned = []
     for group in range(GROUPS):
         two, four, six, low = near[group]
-        e_two, e_four, e_six, high = wrapped[group]
+        e_two, e_six, high = wrapped[group]
         if group:
-            low, high = once((low, high), results[-1][6])
+            low, high, e_six = once((low, high, e_six), results[-1][6])
         else:
             low, high = once((low, high), near[1][0])
+        e_four = along(e_six, [(i + 2, i) for i in range(4)])
         beside = shared(low, two, four, six, first_core, every)
         e_beside = shared(high, e_two, e_four, e_six, first_core, few)
         result = attention_terms(
@@ -513,27 +517,22 @@
             odd, e_odd = once((odd, e_odd), *returned[-1][0], returned[-1][2][0], e_merged)
         got = along(odd, every)
         e_got = along(e_odd, few)
-        direct = group == 0
-        two, four, six, e_two, e_four, e_six = combined(place, even, got, e_even, e_got, half if direct else f32)
+        if group:
+            kernel_terms = exchanged(jnp.concatenate([r[6] for r in (*results, result)], axis=2), steps[:2])
+            got, e_got = once((got, e_got), kernel_terms)
+        two, four, six, e_two, e_four, e_six = combined(place, even, got, e_even, e_got)
         meta = once(meta, two)
         sent_two = along(two, ring_pairs(count, -2))
-        if direct:
-            sent_four = along(four, ring_pairs(count, -4))
-        else:
-            six = (six + along(four, ring_pairs(count, 2)).astype(f32)).astype(half)
+        sent_four = along(four, ring_pairs(count, -4))
         sent_six = along(six, ring_pairs(count, -6))
         e_sent_two = along(e_two, wrapped_back(count, 2))
         e_six = (e_six + along(e_four, [(i, i + 2) for i in range(4)]).astype(f32)).astype(half)
         e_merged = e_six
         e_sent_six = along(e_six, wrapped_back(count, 6))
-        sent = (sent_two, sent_four, sent_six) if direct else (sent_two, sent_six)
         results.append(result)
-        returned.append((sent, got, (e_sent_two, e_sent_six)))
-        last_two = two
-
-    kernel_terms = jnp.concatenate([r[6] for r in results], axis=2)
-    first_sent = (returned[-1][0][0], returned[-1][2][0])
-    kernel_grad = summed_over(kernel_terms, ("ctx", "dp"), {2: (last_two,), 4: first_sent})
+        returned.append(((sent_two, sent_four, sent_six), got, (e_sent_two, e_sent_six)))
+
+    kernel_grad = exchanged(once(kernel_terms, sent_two, sent_four, sent_six, e_sent_two, e_merged), steps[2:])
 
     def after_rows(heads_of):
         low, high = heads_of
@@ -541,7 +540,7 @@
         next_high = along(high, up)
         return jnp.stack([jnp.where(is_last, high, next_low), next_high], axis=-3)
 
-    dq = once(jnp.concatenate([r[0] for r in results], axis=1), *first_sent)
+    dq = once(jnp.concatenate([r[0] for r in results], axis=1), sent_two, sent_six)
     q_after = after_rows((dq[:PAD], dq[HALF : HALF + PAD]))
     wide = min(WIDE, width)
     spec = pl.BlockSpec((rows, wide), lambda h: (0, h))

time: 334 us -> 352 us (1.054)
  waiting for transfers between devices: 119 us -> 133 us
    ppermute x39, waiting for transfers between devices: 72.7 us -> 109 us  [along(): return lax.ppermute(x, 'ctx', pairs)]
    ppermute x8, waiting for transfers between devices: 46.3 us -> 23.4 us  [exchanged(): lax.ppermute(x, axis, [(i, i ^ step) for i in range(lax.axis_size(axis))])]
    ppermute x39, starting transfers between devices: 94.2 us -> 111 us  [along(): return lax.ppermute(x, 'ctx', pairs)]
    ppermute x8, starting transfers between devices: 26.9 us -> 12 us  [exchanged(): lax.ppermute(x, axis, [(i, i ^ step) for i in range(lax.axis_size(axis))])]
  transfers between devices with their start and end apart: 47 -> 47, of which waited for: 20 -> 16; matrix products, arithmetic and copies ran while one was open for 6% -> 6% of each run, Pallas kernels for 17% -> 16%
where the time goes in v1:
time: 352 us; the launch traced here: 349 us
  waiting for transfers between devices  133 us (38%)
  starting transfers between devices  123 us (35%)
  Pallas kernels  66.7 us (19%)
  other arithmetic  17.2 us (5%)
  local copies, waits for them, and re-layouts  8.37 us (2%)
    ppermute x39, starting transfers between devices, along(): return lax.ppermute(x, 'ctx', pairs)  111 us
    ppermute x39, waiting for transfers between devices, along(): return lax.ppermute(x, 'ctx', pairs)  109 us
    pallas_call x2, Pallas kernels, attention_terms(): pl.pallas_call(attention_kernel, grid=(heads,), in_specs=[smem, whole((KE...  49.8 us
    ppermute x8, waiting for transfers between devices, exchanged(): lax.ppermute(x, axis, [(i, i ^ step) for i in range(lax.axis_size(axis))])  23.4 us
    ppermute x8, starting transfers between devices, exchanged(): lax.ppermute(x, axis, [(i, i ^ step) for i in range(lax.axis_size(axis))])  12 us
    pallas_call x2, Pallas kernels, combined(): pl.pallas_call(combine_kernel, grid=(channels // wide,), in_specs=[pl.Blo...  7.72 us
    another operation x8, other arithmetic, shared(): jnp.stack([jnp.where(first_core, own, from_two), jnp.where(first_core, fr...  7.15 us
  transfers between devices with their start and end apart: 47, of which 16 were waited for; matrix products, arithmetic and copies ran while one was open for 6% of the time, Pallas kernels for 16%

profile of v1, /device:TPU:8, one launch (start us, length us, event | category | flops | bytes accessed | tf_op | source)
XLA Modules:
  0.0 349.3 jit_solution(14698764338119599110)
XLA Ops:
  4.3 3.2 collective-permute-start.2
  11.6 3.0 collective-permute-start.4
  21.0 9.1 %collective-permute-done.4.six = bf16[2,128,1024]{2,1,0:T(8,128)(2,1)S(1)} collective-permute-done((bf16[2,128,1024]{2,1,0:T(8,128)(2,1)}, bf16[2,128,1024]{2,1,0:T(8,128)(2,1)S(1)}, u32[]{:S(2)}, u32[]{:S(2)}) %collective-permute-start.4) | collective-permute-done | bytes 524320 | tf_op jit(solution)/shard_map/ppermute | solution.py:29
  33.0 7.5 %collective-permute-done.9.e_six = bf16[2,128,1024]{2,1,0:T(8,128)(2,1)S(1)} collective-permute-done((bf16[2,128,1024]{2,1,0:T(8,128)(2,1)}, bf16[2,128,1024]{2,1,0:T(8,128)(2,1)S(1)}, u32[]{:S(2)}, u32[]{:S(2)}) %collective-permute-start.9) | collective-permute-done | bytes 524320 | tf_op jit(solution)/shard_map/ppermute | solution.py:29
  40.4 2.7 collective-permute-start.10
  45.5 6.2 %collective-permute-done.5.four = bf16[2,128,1024]{2,1,0:T(8,128)(2,1)S(1)} collective-permute-done((bf16[2,128,1024]{2,1,0:T(8,128)(2,1)S(1)}, bf16[2,128,1024]{2,1,0:T(8,128)(2,1)S(1)}, u32[]{:S(2)}, u32[]{:S(2)}) %collective-permute-start.5) | collective-permute-done | bytes 524320 | tf_op jit(solution)/shard_map/ppermute | solution.py:29
  54.4 8.5 %collective-permute-done.10.e_four = bf16[2,128,1024]{2,1,0:T(8,128)(2,1)} collective-permute-done((bf16[2,128,1024]{2,1,0:T(8,128)(2,1)S(1)}, bf16[2,128,1024]{2,1,0:T(8,128)(2,1)}, u32[]{:S(2)}, u32[]{:S(2)}) %collective-permute-start.10) | collective-permute-done | bytes 524320 | tf_op jit(solution)/shard_map/ppermute | solution.py:29
  65.5 2.0 collective-permute-start.11
  72.4 24.8 %attention.2 = (f32[256,1024]{1,0:T(8,128)S(1)}, f32[2,256,1024]{2,1,0:T(8,128)}, bf16[3,2,128,1024]{3,2,1,0:T(8,128)(2,1)}, f32[3,2,128,1024]{3,2,1,0:T(8,128)}...) custom-call(s32[13]{0:T(128)S(1)} %pad_add_fusion.2.meta, ...), custom_call_target="tpu_custom_call" | custom-call | flops 26843545600 | bytes 25165824 | tf_op jit(solution)/shard_map/attention/pallas_call | solution.py:307
  97.2 17.7 %collective-permute-start.19 = (bf16[2,128,1024]{2,1,0:T(8,128)(2,1)S(1)}, bf16[2,128,1024]{2,1,0:T(8,128)(2,1)S(1)}, u32[]{:S(2)}, u32[]{:S(2)}) collective-permute-start(bf16[2,128,1024]{2,1,0:T(8,128)(2,1)S(1)} %collective-permute-done.16.e_six), channel_id=1, source_target_pairs={{2,0},{3,1},{4,2},{5,3},{66,64},{67,65},{68,66},{69,67},{130,128},... | collective-permute-start | bytes 1572872 | tf_op jit(solution)/shard_map/ppermute | solution.py:29
  115.3 2.4 collective-permute-start.13
  117.6 18.8 %collective-permute-done.14.four = bf16[2,128,1024]{2,1,0:T(8,128)(2,1)S(1)} collective-permute-done((bf16[2,128,1024]{2,1,0:T(8,128)(2,1)}, bf16[2,128,1024]{2,1,0:T(8,128)(2,1)S(1)}, u32[]{:S(2)}, u32[]{:S(2)}) %collective-permute-start.14) | collective-permute-done | bytes 524320 | tf_op jit(solution)/shard_map/ppermute | solution.py:29
  142.9 3.8 %combine.2 = (bf16[2,128,1024]{2,1,0:T(8,128)(2,1)S(1)}, bf16[2,128,1024]{2,1,0:T(8,128)(2,1)S(1)}, bf16[2,128,1024]{2,1,0:T(8,128)(2,1)S(1)}, bf16[2,128,1024]{...) custom-call(s32[1]{0:T(128)} %bitcast.meta, ...), custom_call_target="tpu_custom_call" | custom-call | tf_op jit(solution)/shard_map/combine/pallas_call | solution.py:398
  148.6 2.1 collective-permute-start.21
  150.8 23.4 %collective-permute-done.25 = bf16[2,128,1024]{2,1,0:T(8,128)(2,1)S(1)} collective-permute-done((bf16[2,128,1024]{2,1,0:T(8,128)(2,1)S(1)}, bf16[2,128,1024]{2,1,0:T(8,128)(2,1)S(1)}, u32[]{:S(2)}, u32[]{:S(2)}) %collective-permute-start.25) | collective-permute-done | bytes 524320 | tf_op jit(solution)/shard_map/ppermute | solution.py:29
  176.3 25.0 %attention.3 = (f32[256,1024]{1,0:T(8,128)S(1)}, f32[2,256,1024]{2,1,0:T(8,128)}, bf16[3,2,128,1024]{3,2,1,0:T(8,128)(2,1)}, f32[3,2,128,1024]{3,2,1,0:T(8,128)}...) custom-call(s32[13]{0:T(128)S(1)} %pad_add_fusion.2.meta, ...), custom_call_target="tpu_custom_call" | custom-call | flops 26843545600 | bytes 25165824 | tf_op jit(solution)/shard_map/attention/pallas_call | solution.py:307
  201.4 2.4 collective-permute-start.27
  203.9 3.2 collective-permute-done.28
  207.2 7.1 %collective-permute-start.29 = (f32[3,4,2048]{2,1,0:T(4,128)S(1)}, f32[3,4,2048]{2,1,0:T(4,128)S(1)}, u32[]{:S(2)}, u32[]{:S(2)}) collective-permute-start(f32[3,4,2048]{2,1,0:T(4,128)S(1)} %add.214), channel_id=1, source_target_pairs={{0,2},{1,3},{2,0},{3,1},{4,6},{5,7},{6,4},{7,5},{8,10},{9,11},{10,... | collective-permute-start | bytes 294920 | tf_op jit(solution)/shard_map/ppermute | solution.py:64
  214.3 3.1 collective-permute-done.29
  218.6 3.9 %combine.3 = (bf16[2,128,1024]{2,1,0:T(8,128)(2,1)S(1)}, bf16[2,128,1024]{2,1,0:T(8,128)(2,1)S(1)}, bf16[2,128,1024]{2,1,0:T(8,128)(2,1)S(1)}, bf16[2,128,1024]{...) custom-call(s32[1]{0:T(128)} %bitcast.meta, ...), custom_call_target="tpu_custom_call" | custom-call | tf_op jit(solution)/shard_map/combine/pallas_call | solution.py:398
  224.4 2.1 collective-permute-start.30
  229.3 31.0 %collective-permute-done.36 = bf16[2,128,1024]{2,1,0:T(8,128)(2,1)S(1)} collective-permute-done((bf16[2,128,1024]{2,1,0:T(8,128)(2,1)S(1)}, bf16[2,128,1024]{2,1,0:T(8,128)(2,1)S(1)}, u32[]{:S(2)}, u32[]{:S(2)}) %collective-permute-start.36) | collective-permute-done | bytes 524320 | tf_op jit(solution)/shard_map/ppermute | solution.py:29
  262.0 6.1 %collective-permute-done.41 = f32[3,4,2048]{2,1,0:T(4,128)S(1)} collective-permute-done((f32[3,4,2048]{2,1,0:T(4,128)S(1)}, f32[3,4,2048]{2,1,0:T(4,128)S(1)}, u32[]{:S(2)}, u32[]{:S(2)}) %collective-permute-start.41) | collective-permute-done | bytes 98336 | tf_op jit(solution)/shard_map/ppermute | solution.py:64
  268.2 43.7 %collective-permute-start.37 = (bf16[2,128,1024]{2,1,0:T(8,128)(2,1)S(1)}, bf16[2,128,1024]{2,1,0:T(8,128)(2,1)S(1)}, u32[]{:S(2)}, u32[]{:S(2)}) collective-permute-start(bf16[2,128,1024]{2,1,0:T(8,128)(2,1)S(1)} %add_convert_fusion), channel_id=1, source_target_pairs={{0,58},{1,59},{2,60},{3,61},{4,62},{5,63},{64,122},{65,123},{66,12... | collective-permute-start | bytes 1572872 | tf_op jit(solution)/shard_map/ppermute | solution.py:29
  312.3 5.3 %collective-permute-done.43 = f32[3,4,2048]{2,1,0:T(4,128)S(1)} collective-permute-done((f32[3,4,2048]{2,1,0:T(4,128)S(1)}, f32[3,4,2048]{2,1,0:T(4,128)S(1)}, u32[]{:S(2)}, u32[]{:S(2)}) %collective-permute-start.43) | collective-permute-done | bytes 98336 | tf_op jit(solution)/shard_map/ppermute | solution.py:64
  320.6 5.6 %collective-permute-done.44 = f32[3,4,2048]{2,1,0:T(4,128)S(1)} collective-permute-done((f32[3,4,2048]{2,1,0:T(4,128)S(1)}, f32[3,4,2048]{2,1,0:T(4,128)S(1)}, u32[]{:S(2)}, u32[]{:S(2)}) %collective-permute-start.44) | collective-permute-done | bytes 98336 | tf_op jit(solution)/shard_map/ppermute | solution.py:64
  330.7 2.4 collective-permute-start.33
  333.2 2.8 collective-permute-start.46
  338.0 2.3 query_finish.1
  342.4 3.5 finish.2
  345.8 3.4 finish.3
  (165 shorter events, 59.5 us)
Async XLA Ops:
  1.6 18.4 %collective-permute-start = (bf16[8,2048]{1,0:T(8,128)(2,1)S(1)}, bf16[8,2048]{1,0:T(8,128)(2,1)S(1)}, u32[]{:S(2)}, u32[]{:S(2)}) collective-permute-start(bf16[8,2048]{1,0:T(8,128)(2,1)S(1)} %get-tuple-element.110), channel_id=1, source_target_pairs={{0,1},{1,2},{2,3},{3,4},{4,5},{5,6},{6,7},{7,8},{8,9},{9,10},{10,1... | collective-permute-start | bytes 98312 | tf_op jit(solution)/shard_map/ppermute | solution.py:29
  11.6 18.5 %collective-permute-start.4 = (bf16[2,128,1024]{2,1,0:T(8,128)(2,1)}, bf16[2,128,1024]{2,1,0:T(8,128)(2,1)S(1)}, u32[]{:S(2)}, u32[]{:S(2)}) collective-permute-start(bf16[2,128,1024]{2,1,0:T(8,128)(2,1)} %pad_maximum_fusion.5), channel_id=1, source_target_pairs={{0,6},{1,7},{2,8},{3,9},{4,10},{5,11},{6,12},{7,13},{8,14},{9,15},... | collective-permute-start | bytes 1572872 | tf_op jit(solution)/shard_map/ppermute | solution.py:29
  15.5 25.0 %collective-permute-start.9 = (bf16[2,128,1024]{2,1,0:T(8,128)(2,1)}, bf16[2,128,1024]{2,1,0:T(8,128)(2,1)S(1)}, u32[]{:S(2)}, u32[]{:S(2)}) collective-permute-start(bf16[2,128,1024]{2,1,0:T(8,128)(2,1)} %pad_maximum_fusion.6), channel_id=1, source_target_pairs={{58,0},{59,1},{60,2},{61,3},{62,4},{63,5},{122,64},{123,65},{124,6... | collective-permute-start | bytes 1572872 | tf_op jit(solution)/shard_map/ppermute | solution.py:29
  20.0 25.5 %collective-permute-start.3 = (bf16[2,128,1024]{2,1,0:T(8,128)(2,1)}, bf16[2,128,1024]{2,1,0:T(8,128)(2,1)S(1)}, u32[]{:S(2)}, u32[]{:S(2)}) collective-permute-start(bf16[2,128,1024]{2,1,0:T(8,128)(2,1)} %pad_maximum_fusion.5), channel_id=1, source_target_pairs={{0,2},{1,3},{2,4},{3,5},{4,6},{5,7},{6,8},{7,9},{8,10},{9,11},{10,... | collective-permute-start | bytes 1572872 | tf_op jit(solution)/shard_map/ppermute | solution.py:29
  20.3 34.1 %collective-permute-start.8 = (bf16[2,128,1024]{2,1,0:T(8,128)(2,1)}, bf16[2,128,1024]{2,1,0:T(8,128)(2,1)S(1)}, u32[]{:S(2)}, u32[]{:S(2)}) collective-permute-start(bf16[2,128,1024]{2,1,0:T(8,128)(2,1)} %pad_maximum_fusion.6), channel_id=1, source_target_pairs={{62,0},{63,1},{126,64},{127,65},{190,128},{191,129},{254,192},{255... | collective-permute-start | bytes 1572872 | tf_op jit(solution)/shard_map/ppermute | solution.py:29
  30.1 21.5 %collective-permute-start.5 = (bf16[2,128,1024]{2,1,0:T(8,128)(2,1)S(1)}, bf16[2,128,1024]{2,1,0:T(8,128)(2,1)S(1)}, u32[]{:S(2)}, u32[]{:S(2)}) collective-permute-start(bf16[2,128,1024]{2,1,0:T(8,128)(2,1)S(1)} %collective-permute-done.4.six), channel_id=1, source_target_pairs={{0,62},{1,63},{2,0},{3,1},{4,2},{5,3},{6,4},{7,5},{8,6},{9,7},{10,... | collective-permute-start | bytes 1572872 | tf_op jit(solution)/shard_map/ppermute | solution.py:29
  40.4 22.5 %collective-permute-start.10 = (bf16[2,128,1024]{2,1,0:T(8,128)(2,1)S(1)}, bf16[2,128,1024]{2,1,0:T(8,128)(2,1)}, u32[]{:S(2)}, u32[]{:S(2)}) collective-permute-start(bf16[2,128,1024]{2,1,0:T(8,128)(2,1)S(1)} %collective-permute-done.9.e_six), channel_id=1, source_target_pairs={{2,0},{3,1},{4,2},{5,3},{66,64},{67,65},{68,66},{69,67},{130,128},... | collective-permute-start | bytes 1572872 | tf_op jit(solution)/shard_map/ppermute | solution.py:29
  54.4 16.4 %collective-permute-start.7 = (bf16[3,2,128,1024]{3,2,1,0:T(8,128)(2,1)}, bf16[3,2,128,1024]{3,2,1,0:T(8,128)(2,1)}, u32[]{:S(2)}, u32[]{:S(2)}) collective-permute-start(bf16[3,2,128,1024]{3,2,1,0:T(8,128)(2,1)} %pad_maximum_fusion.1), channel_id=1, source_target_pairs={{0,1},{1,0},{2,3},{3,2},{4,5},{5,4},{6,7},{7,6},{8,9},{9,8},{10,11... | collective-permute-start | bytes 4718600 | tf_op jit(solution)/shard_map/ppermute | solution.py:29
  68.7 68.1 %collective-permute-start.18 = (bf16[2,128,1024]{2,1,0:T(8,128)(2,1)}, bf16[2,128,1024]{2,1,0:T(8,128)(2,1)S(1)}, u32[]{:S(2)}, u32[]{:S(2)}) collective-permute-start(bf16[2,128,1024]{2,1,0:T(8,128)(2,1)} %get-tuple-element.64), channel_id=1, source_target_pairs={{62,0},{63,1},{126,64},{127,65},{190,128},{191,129},{254,192},{255... | collective-permute-start | bytes 1572872 | tf_op jit(solution)/shard_map/ppermute | solution.py:29
  69.4 27.8 %collective-permute-start.16 = (bf16[2,128,1024]{2,1,0:T(8,128)(2,1)}, bf16[2,128,1024]{2,1,0:T(8,128)(2,1)S(1)}, u32[]{:S(2)}, u32[]{:S(2)}) collective-permute-start(bf16[2,128,1024]{2,1,0:T(8,128)(2,1)} %get-tuple-element.64), channel_id=1, source_target_pairs={{58,0},{59,1},{60,2},{61,3},{62,4},{63,5},{122,64},{123,65},{124,6... | collective-permute-start | bytes 1572872 | tf_op jit(solution)/shard_map/ppermute | solution.py:29
  70.7 44.5 %collective-permute-start.15 = (bf16[2,128,1024]{2,1,0:T(8,128)(2,1)}, bf16[2,128,1024]{2,1,0:T(8,128)(2,1)S(1)}, u32[]{:S(2)}, u32[]{:S(2)}) collective-permute-start(bf16[2,128,1024]{2,1,0:T(8,128)(2,1)} %get-tuple-element.62), channel_id=1, source_target_pairs={{0,6},{1,7},{2,8},{3,9},{4,10},{5,11},{6,12},{7,13},{8,14},{9,15},... | collective-permute-start | bytes 1572872 | tf_op jit(solution)/shard_map/ppermute | solution.py:29
  70.8 65.6 %collective-permute-start.14 = (bf16[2,128,1024]{2,1,0:T(8,128)(2,1)}, bf16[2,128,1024]{2,1,0:T(8,128)(2,1)S(1)}, u32[]{:S(2)}, u32[]{:S(2)}) collective-permute-start(bf16[2,128,1024]{2,1,0:T(8,128)(2,1)} %get-tuple-element.62), channel_id=1, source_target_pairs={{0,4},{1,5},{2,6},{3,7},{4,8},{5,9},{6,10},{7,11},{8,12},{9,13},{1... | collective-permute-start | bytes 1572872 | tf_op jit(solution)/shard_map/ppermute | solution.py:29
  97.2 41.1 %collective-permute-start.19 = (bf16[2,128,1024]{2,1,0:T(8,128)(2,1)S(1)}, bf16[2,128,1024]{2,1,0:T(8,128)(2,1)S(1)}, u32[]{:S(2)}, u32[]{:S(2)}) collective-permute-start(bf16[2,128,1024]{2,1,0:T(8,128)(2,1)S(1)} %collective-permute-done.16.e_six), channel_id=1, source_target_pairs={{2,0},{3,1},{4,2},{5,3},{66,64},{67,65},{68,66},{69,67},{130,128},... | collective-permute-start | bytes 1572872 | tf_op jit(solution)/shard_map/ppermute | solution.py:29
  115.0 26.7 %collective-permute-start.12 = (bf16[3,2,128,1024]{3,2,1,0:T(8,128)(2,1)}, bf16[3,2,128,1024]{3,2,1,0:T(8,128)(2,1)S(1)}, u32[]{:S(2)}, u32[]{:S(2)}) collective-permute-start(bf16[3,2,128,1024]{3,2,1,0:T(8,128)(2,1)} %get-tuple-element.55), channel_id=1, source_target_pairs={{0,1},{1,0},{2,3},{3,2},{4,5},{5,4},{6,7},{7,6},{8,9},{9,8},{10,11... | collective-permute-start | bytes 4718600 | tf_op jit(solution)/shard_map/ppermute | solution.py:29
  115.3 26.5 %collective-permute-start.13 = (bf16[3,2,128,1024]{3,2,1,0:T(8,128)(2,1)}, bf16[3,2,128,1024]{3,2,1,0:T(8,128)(2,1)S(1)}, u32[]{:S(2)}, u32[]{:S(2)}) collective-permute-start(bf16[3,2,128,1024]{3,2,1,0:T(8,128)(2,1)} %get-tuple-element.57), channel_id=1, source_target_pairs={{0,1},{1,0},{2,3},{3,2},{4,5},{5,4},{64,65},{65,64},{66,67},{67,66... | collective-permute-start | bytes 4718600 | tf_op jit(solution)/shard_map/ppermute | solution.py:29
  136.7 38.4 %collective-permute-start.17 = (bf16[3,2,128,1024]{3,2,1,0:T(8,128)(2,1)S(1)}, bf16[3,2,128,1024]{3,2,1,0:T(8,128)(2,1)S(1)}, u32[]{:S(2)}, u32[]{:S(2)}) collective-permute-start(bf16[3,2,128,1024]{3,2,1,0:T(8,128)(2,1)S(1)} %pad_maximum_fusion.3), channel_id=1, source_target_pairs={{0,1},{1,0},{2,3},{3,2},{4,5},{5,4},{6,7},{7,6},{8,9},{9,8},{10,11... | collective-permute-start | bytes 4718600 | tf_op jit(solution)/shard_map/ppermute | solution.py:29
  139.8 36.0 %collective-permute-start.20 = (bf16[3,2,128,1024]{3,2,1,0:T(8,128)(2,1)}, bf16[3,2,128,1024]{3,2,1,0:T(8,128)(2,1)}, u32[]{:S(2)}, u32[]{:S(2)}) collective-permute-start(bf16[3,2,128,1024]{3,2,1,0:T(8,128)(2,1)} %pad_maximum_fusion.4), channel_id=1, source_target_pairs={{0,1},{1,0},{2,3},{3,2},{4,5},{5,4},{64,65},{65,64},{66,67},{67,66... | collective-permute-start | bytes 4718600 | tf_op jit(solution)/shard_map/ppermute | solution.py:29
  146.7 27.5 %collective-permute-start.25 = (bf16[2,128,1024]{2,1,0:T(8,128)(2,1)S(1)}, bf16[2,128,1024]{2,1,0:T(8,128)(2,1)S(1)}, u32[]{:S(2)}, u32[]{:S(2)}) collective-permute-start(bf16[2,128,1024]{2,1,0:T(8,128)(2,1)S(1)} %get-tuple-element.73), channel_id=1, source_target_pairs={{0,2},{1,3},{2,4},{3,5},{64,66},{65,67},{66,68},{67,69},{128,130},... | collective-permute-start | bytes 1572872 | tf_op jit(solution)/shard_map/ppermute | solution.py:29
  148.6 52.6 %collective-permute-start.21 = (bf16[2,128,1024]{2,1,0:T(8,128)(2,1)S(1)}, bf16[2,128,1024]{2,1,0:T(8,128)(2,1)S(1)}, u32[]{:S(2)}, u32[]{:S(2)}) collective-permute-start(bf16[2,128,1024]{2,1,0:T(8,128)(2,1)S(1)} %get-tuple-element.58), channel_id=1, source_target_pairs={{0,62},{1,63},{2,0},{3,1},{4,2},{5,3},{6,4},{7,5},{8,6},{9,7},{10,... | collective-permute-start | bytes 1572872 | tf_op jit(solution)/shard_map/ppermute | solution.py:29
  150.8 50.5 %collective-permute-start.22 = (bf16[2,128,1024]{2,1,0:T(8,128)(2,1)S(1)}, bf16[2,128,1024]{2,1,0:T(8,128)(2,1)S(1)}, u32[]{:S(2)}, u32[]{:S(2)}) collective-permute-start(bf16[2,128,1024]{2,1,0:T(8,128)(2,1)S(1)} %get-tuple-element.69), channel_id=1, source_target_pairs={{0,60},{1,61},{2,62},{3,63},{4,0},{5,1},{6,2},{7,3},{8,4},{9,5},{1... | collective-permute-start | bytes 1572872 | tf_op jit(solution)/shard_map/ppermute | solution.py:29
  174.2 27.1 %collective-permute-start.23 = (bf16[2,128,1024]{2,1,0:T(8,128)(2,1)S(1)}, bf16[2,128,1024]{2,1,0:T(8,128)(2,1)S(1)}, u32[]{:S(2)}, u32[]{:S(2)}) collective-permute-start(bf16[2,128,1024]{2,1,0:T(8,128)(2,1)S(1)} %get-tuple-element.70), channel_id=1, source_target_pairs={{0,58},{1,59},{2,60},{3,61},{4,62},{5,63},{6,0},{7,1},{8,2},{9,3},... | collective-permute-start | bytes 1572872 | tf_op jit(solution)/shard_map/ppermute | solution.py:29
  175.1 26.1 %collective-permute-start.24 = (bf16[2,128,1024]{2,1,0:T(8,128)(2,1)S(1)}, bf16[2,128,1024]{2,1,0:T(8,128)(2,1)S(1)}, u32[]{:S(2)}, u32[]{:S(2)}) collective-permute-start(bf16[2,128,1024]{2,1,0:T(8,128)(2,1)S(1)} %get-tuple-element.71), channel_id=1, source_target_pairs={{0,62},{1,63},{64,126},{65,127},{128,190},{129,191},{192,254},{193... | collective-permute-start | bytes 1572872 | tf_op jit(solution)/shard_map/ppermute | solution.py:29
  201.3 16.1 %collective-permute-start.26 = (bf16[3,2,128,1024]{3,2,1,0:T(8,128)(2,1)}, bf16[3,2,128,1024]{3,2,1,0:T(8,128)(2,1)S(1)}, u32[]{:S(2)}, u32[]{:S(2)}) collective-permute-start(bf16[3,2,128,1024]{3,2,1,0:T(8,128)(2,1)} %get-tuple-element.74), channel_id=1, source_target_pairs={{0,1},{1,0},{2,3},{3,2},{4,5},{5,4},{6,7},{7,6},{8,9},{9,8},{10,11... | collective-permute-start | bytes 4718600 | tf_op jit(solution)/shard_map/ppermute | solution.py:29
  201.4 16.1 %collective-permute-start.27 = (bf16[3,2,128,1024]{3,2,1,0:T(8,128)(2,1)}, bf16[3,2,128,1024]{3,2,1,0:T(8,128)(2,1)S(1)}, u32[]{:S(2)}, u32[]{:S(2)}) collective-permute-start(bf16[3,2,128,1024]{3,2,1,0:T(8,128)(2,1)} %get-tuple-element.75), channel_id=1, source_target_pairs={{0,1},{1,0},{2,3},{3,2},{4,5},{5,4},{64,65},{65,64},{66,67},{67,66... | collective-permute-start | bytes 4718600 | tf_op jit(solution)/shard_map/ppermute | solution.py:29
  222.5 37.8 %collective-permute-start.36 = (bf16[2,128,1024]{2,1,0:T(8,128)(2,1)S(1)}, bf16[2,128,1024]{2,1,0:T(8,128)(2,1)S(1)}, u32[]{:S(2)}, u32[]{:S(2)}) collective-permute-start(bf16[2,128,1024]{2,1,0:T(8,128)(2,1)S(1)} %get-tuple-element.87), channel_id=1, source_target_pairs={{0,2},{1,3},{2,4},{3,5},{64,66},{65,67},{66,68},{67,69},{128,130},... | collective-permute-start | bytes 1572872 | tf_op jit(solution)/shard_map/ppermute | solution.py:29
  224.4 37.4 %collective-permute-start.30 = (bf16[2,128,1024]{2,1,0:T(8,128)(2,1)S(1)}, bf16[2,128,1024]{2,1,0:T(8,128)(2,1)S(1)}, u32[]{:S(2)}, u32[]{:S(2)}) collective-permute-start(bf16[2,128,1024]{2,1,0:T(8,128)(2,1)S(1)} %get-tuple-element.80), channel_id=1, source_target_pairs={{0,62},{1,63},{2,0},{3,1},{4,2},{5,3},{6,4},{7,5},{8,6},{9,7},{10,... | collective-permute-start | bytes 1572872 | tf_op jit(solution)/shard_map/ppermute | solution.py:29
  226.6 35.3 %collective-permute-start.31 = (bf16[2,128,1024]{2,1,0:T(8,128)(2,1)S(1)}, bf16[2,128,1024]{2,1,0:T(8,128)(2,1)S(1)}, u32[]{:S(2)}, u32[]{:S(2)}) collective-permute-start(bf16[2,128,1024]{2,1,0:T(8,128)(2,1)S(1)} %get-tuple-element.81), channel_id=1, source_target_pairs={{0,58},{1,59},{2,60},{3,61},{4,62},{5,63},{6,0},{7,1},{8,2},{9,3},... | collective-permute-start | bytes 1572872 | tf_op jit(solution)/shard_map/ppermute | solution.py:29
  226.6 35.3 %collective-permute-start.35 = (bf16[2,128,1024]{2,1,0:T(8,128)(2,1)S(1)}, bf16[2,128,1024]{2,1,0:T(8,128)(2,1)S(1)}, u32[]{:S(2)}, u32[]{:S(2)}) collective-permute-start(bf16[2,128,1024]{2,1,0:T(8,128)(2,1)S(1)} %get-tuple-element.85), channel_id=1, source_target_pairs={{0,62},{1,63},{64,126},{65,127},{128,190},{129,191},{192,254},{193... | collective-permute-start | bytes 1572872 | tf_op jit(solution)/shard_map/ppermute | solution.py:29
  227.5 34.4 %collective-permute-start.38 = (bf16[2,128,1024]{2,1,0:T(8,128)(2,1)S(1)}, bf16[2,128,1024]{2,1,0:T(8,128)(2,1)S(1)}, u32[]{:S(2)}, u32[]{:S(2)}) collective-permute-start(bf16[2,128,1024]{2,1,0:T(8,128)(2,1)S(1)} %get-tuple-element.88), channel_id=1, source_target_pairs={{0,60},{1,61},{2,62},{3,63},{4,0},{5,1},{6,2},{7,3},{8,4},{9,5},{1... | collective-permute-start | bytes 1572872 | tf_op jit(solution)/shard_map/ppermute | solution.py:29
  260.3 57.4 %collective-permute-start.34 = (bf16[2,128,1024]{2,1,0:T(8,128)(2,1)S(1)}, bf16[2,128,1024]{2,1,0:T(8,128)(2,1)S(1)}, u32[]{:S(2)}, u32[]{:S(2)}) collective-permute-start(bf16[2,128,1024]{2,1,0:T(8,128)(2,1)S(1)} %copy-done.8), channel_id=1, source_target_pairs={{0,58},{1,59},{2,60},{3,61},{4,62},{5,63},{64,122},{65,123},{66,12... | collective-permute-start | bytes 1572872 | tf_op jit(solution)/shard_map/ppermute | solution.py:29
  268.1 43.8 %collective-permute-start.42 = (f32[3,4,2048]{2,1,0:T(4,128)S(1)}, f32[3,4,2048]{2,1,0:T(4,128)S(1)}, u32[]{:S(2)}, u32[]{:S(2)}) collective-permute-start(f32[3,4,2048]{2,1,0:T(4,128)S(1)} %add.229), channel_id=1, source_target_pairs={{0,8},{1,9},{2,10},{3,11},{4,12},{5,13},{6,14},{7,15},{8,0},{9,1},... | collective-permute-start | bytes 294920 | tf_op jit(solution)/shard_map/ppermute | solution.py:64
  268.2 59.6 %collective-permute-start.37 = (bf16[2,128,1024]{2,1,0:T(8,128)(2,1)S(1)}, bf16[2,128,1024]{2,1,0:T(8,128)(2,1)S(1)}, u32[]{:S(2)}, u32[]{:S(2)}) collective-permute-start(bf16[2,128,1024]{2,1,0:T(8,128)(2,1)S(1)} %add_convert_fusion), channel_id=1, source_target_pairs={{0,58},{1,59},{2,60},{3,61},{4,62},{5,63},{64,122},{65,123},{66,12... | collective-permute-start | bytes 1572872 | tf_op jit(solution)/shard_map/ppermute | solution.py:29
  (26 other events, 266.3 us)
